TPU v7x, 512 devices: a whole 4x8x8 slice. The times are simulated.
512 devices in a mesh: node: 8 (over z), outer: 64 (over x, y, core).
Axes of the slice: x: 4, y: 8, z: 8, core: 2. Of those that a mesh axis runs over, the one named last changes fastest.
Arguments:
- tokens: bfloat16 [16384, 2048], P('outer', 'node'), may hold values from -6 to 6
- cotangent: bfloat16 [16384, 2048], P('outer', 'node'), may hold values from -6 to 6
- gate: float32 [16384], P('outer'), may hold values from 0.2 to 1
- expert_ids: int32 [16384, 1], P('outer'), may hold values from 0 to 63; in each aligned block of 256 rows (0 to 255, 256 to 511, ...) at most 8 rows name the same one
- dense_in: bfloat16 [2048, 4096], P('outer', 'node'), may hold values from -0.125 to 0.125
- dense_out: bfloat16 [4096, 2048], P('node', 'outer'), may hold values from -0.09375 to 0.09375
- expert_in: bfloat16 [64, 2048, 4096], P('outer', None, 'node'), may hold values from -0.125 to 0.125
- expert_out: bfloat16 [64, 4096, 2048], P('outer', 'node'), may hold values from -0.09375 to 0.09375
Outputs:
- mixed: bfloat16 [16384, 2048], P('outer', 'node')
- input_grad: bfloat16 [16384, 2048], P('outer', 'node')
Inputs may be any that keep to these rules, and one draw needn't show every extreme that they name: `expert_ids`: within the tokens of one index of outer (aligned blocks of 256 rows) no expert is named by more than 8 tokens, and in some blocks one is named by exactly 8; every expert is named somewhere.
All inputs are finite; a program needn't handle non-finite values.
Results may differ from a plain program's by a relative error of at most 0.015.
Values may be sent and summed in bfloat16 or wider, within the bound.
No kernel may reach another device: no remote copies, remote signals or barrier semaphores. Data moves between devices by JAX's collectives and lax.ppermute only.
A program may use at most 64 MiB of HBM per device.

v0:
```python
import jax
import jax.numpy as jnp
from jax import lax
from jax.sharding import PartitionSpec as P


def gelu_value(v):
    return 0.5 * v * (1.0 + lax.erf(v * 0.7071067811865476))


def gelu_prime(v):
    return (
        0.5 * (1.0 + lax.erf(v * 0.7071067811865476))
        + v * jnp.exp(-0.5 * v * v) * 0.3989422804014327
    )


def contract_last(left, right):
    return lax.dot_general(
        left, right, (((1,), (1,)), ((), ())), preferred_element_type=jnp.float32
    )


def body(tokens, cotangent, gate, expert_ids, dense_in, dense_out, expert_in, expert_out):
    full_x, full_c = (
        lax.all_gather(tokens, "node", axis=1, tiled=True),
        lax.all_gather(cotangent, "node", axis=1, tiled=True),
    )
    weight_in, weight_out = (
        lax.all_gather(dense_in, "outer", axis=0, tiled=True),
        lax.all_gather(dense_out, "outer", axis=1, tiled=True),
    )
    tok_count = tokens.shape[0]
    width = full_x.shape[1]
    expert_count = lax.axis_size("outer") * expert_in.shape[0]
    capacity = max(2, 2 * tok_count // lax.axis_size("outer"))
    labels = jnp.arange(expert_count, dtype=jnp.int32)
    routed = expert_ids[:, 0]
    onehot = (routed[:, None] == labels[None, :]).astype(jnp.int32)
    ranks = jnp.sum((jnp.cumsum(onehot, axis=0) - 1) * onehot, axis=1)
    slot_of = routed * capacity + ranks
    local_in = expert_in[0]
    local_out = expert_out[0]
    send_x = jnp.zeros((expert_count * capacity, width), jnp.bfloat16).at[slot_of].set(full_x)
    send_c = jnp.zeros((expert_count * capacity, width), jnp.bfloat16).at[slot_of].set(full_c)
    send_x = send_x.reshape(expert_count, capacity, width)
    send_c = send_c.reshape(expert_count, capacity, width)
    rows_x = lax.all_to_all(send_x, "outer", split_axis=0, concat_axis=0, tiled=True)
    rows_c = lax.all_to_all(send_c, "outer", split_axis=0, concat_axis=0, tiled=True)
    dims_of = rows_x.shape
    flat_x = rows_x.reshape(-1, dims_of[2])
    flat_c = rows_c.reshape(-1, dims_of[2])
    pre_act = jnp.dot(flat_x, local_in, preferred_element_type=jnp.float32)
    hidden = gelu_value(pre_act).astype(jnp.bfloat16)
    part_out = jnp.dot(hidden, local_out, preferred_element_type=jnp.float32).astype(jnp.bfloat16)
    grad_hid = contract_last(flat_c, local_out)
    dpre = (grad_hid * gelu_prime(pre_act)).astype(jnp.bfloat16)
    part_back = contract_last(dpre, local_in).astype(jnp.bfloat16)
    back_out = lax.all_to_all(
        part_out.reshape(dims_of), "outer", split_axis=0, concat_axis=0, tiled=True
    )
    back_grad = lax.all_to_all(
        part_back.reshape(dims_of), "outer", split_axis=0, concat_axis=0, tiled=True
    )
    dense_pre = jnp.dot(full_x, weight_in, preferred_element_type=jnp.float32)
    dense_hidden = gelu_value(dense_pre).astype(jnp.bfloat16)
    dense_fwd = jnp.dot(dense_hidden, weight_out, preferred_element_type=jnp.float32)
    dense_grad = contract_last(full_c, weight_out)
    dense_dpre = (dense_grad * gelu_prime(dense_pre)).astype(jnp.bfloat16)
    dense_bwd = contract_last(dense_dpre, weight_in)
    routed_out = jnp.take(back_out.reshape(-1, width), slot_of, axis=0).astype(jnp.float32)
    routed_back = jnp.take(back_grad.reshape(-1, width), slot_of, axis=0).astype(jnp.float32)
    weight = gate[:, None]
    sum_out, sum_back = (
        lax.psum_scatter(
            (dense_fwd + weight * routed_out).astype(jnp.bfloat16),
            "node",
            scatter_dimension=1,
            tiled=True,
        ).astype(jnp.float32),
        lax.psum_scatter(
            (dense_bwd + weight * routed_back).astype(jnp.bfloat16),
            "node",
            scatter_dimension=1,
            tiled=True,
        ).astype(jnp.float32),
    )
    mixed = (tokens.astype(jnp.float32) + sum_out).astype(jnp.bfloat16)
    input_grad = (cotangent.astype(jnp.float32) + sum_back).astype(jnp.bfloat16)
    return (mixed, input_grad)


def solution(mesh):
    placed = (
        P("outer", "node"),
        P("outer", "node"),
        P("outer"),
        P("outer", None),
        P("outer", "node"),
        P("node", "outer"),
        P("outer", None, "node"),
        P("outer", "node", None),
    )
    return jax.shard_map(
        body,
        mesh=mesh,
        in_specs=placed,
        out_specs=(P("outer", "node"), P("outer", "node")),
        check_vma=False,
    )
```

profile of v0, /device:TPU:1, one launch (start us, length us, event | category | flops | bytes accessed | tf_op | source)
XLA Modules:
  0.0 411.4 jit_solution(8735395694601383843)
XLA Ops:
  11.7 43.3 %all-gather.5.cloned.1.call-done = bf16[256,2048]{1,0:T(8,128)(2,1)} async-done(((bf16[256,256]{1,0:T(8,128)(2,1)}), bf16[256,2048]{1,0:T(8,128)(2,1)}) %all-gather.5.cloned.1.call-update) | async-done | bytes 1048592 | tf_op jit(solution)/shard_map/all_gather | solution.py:26
  55.1 4.4 %scatter_custom_fusion = bf16[512,2048]{1,0:T(8,128)(2,1)} fusion(s32[256]{0:T(256)S(1)} %bitcast.67, bf16[256,2048]{1,0:T(8,128)(2,1)} %all-gather.5.cloned.1.call-done, bf16[]{:T(256)} %constant.21.clone.1), kind=kCustom, calls=%fused_computation.33 | custom fusion | bytes 2097664 | tf_op jit(solution)/shard_map/scatter | solution.py:44
  59.5 14.8 %all-to-all-start = ((bf16[64,8,2048]{2,1,0:T(8,128)(2,1)}), bf16[64,8,2048]{2,1,0:T(8,128)(2,1)}, u32[]{:S(2)}, u32[]{:S(2)}) async-start(bf16[64,8,2048]{2,1,0:T(8,128)(2,1)} %bitcast.62), calls=%async_computation | async-start | bytes 4194304 | tf_op jit(solution)/shard_map/all_to_all | solution.py:48
  75.1 40.3 %all-gather.11.cloned.1.call-done = bf16[256,2048]{1,0:T(8,128)(2,1)} async-done(((bf16[256,256]{1,0:T(8,128)(2,1)}), bf16[256,2048]{1,0:T(8,128)(2,1)}) %all-gather.11.cloned.1.call-update) | async-done | bytes 1048592 | tf_op jit(solution)/shard_map/all_gather | solution.py:27
  115.4 4.4 %scatter_custom_fusion.1 = bf16[512,2048]{1,0:T(8,128)(2,1)} fusion(s32[256]{0:T(256)S(1)} %bitcast.68, bf16[256,2048]{1,0:T(8,128)(2,1)} %all-gather.11.cloned.1.call-done, bf16[]{:T(256)} %constant.21.clone.1), kind=kCustom, calls=%fused_computation.31 | custom fusion | bytes 2097664 | tf_op jit(solution)/shard_map/scatter | solution.py:45
  119.8 5.7 %all-to-all-done = bf16[64,8,2048]{2,1,0:T(8,128)(2,1)} async-done(((bf16[64,8,2048]{2,1,0:T(8,128)(2,1)}), bf16[64,8,2048]{2,1,0:T(8,128)(2,1)}, u32[]{:S(2)}, u32[]{:S(2)}) %all-to-all-start) | async-done | bytes 2097184 | tf_op jit(solution)/shard_map/all_to_all | solution.py:48
  125.5 8.0 %all-to-all-start.2 = ((bf16[64,8,2048]{2,1,0:T(8,128)(2,1)}), bf16[64,8,2048]{2,1,0:T(8,128)(2,1)}, u32[]{:S(2)}, u32[]{:S(2)}) async-start(bf16[64,8,2048]{2,1,0:T(8,128)(2,1)} %bitcast.61), calls=%async_computation.3 | async-start | bytes 4194304 | tf_op jit(solution)/shard_map/all_to_all | solution.py:49
  134.0 3.5 fusion.9
  137.5 48.2 %all-to-all-done.2 = bf16[64,8,2048]{2,1,0:T(8,128)(2,1)} async-done(((bf16[64,8,2048]{2,1,0:T(8,128)(2,1)}), bf16[64,8,2048]{2,1,0:T(8,128)(2,1)}, u32[]{:S(2)}, u32[]{:S(2)}) %all-to-all-start.2) | async-done | bytes 2097184 | tf_op jit(solution)/shard_map/all_to_all | solution.py:49
  185.8 6.2 %fusion.1 = bf16[64,8,2048]{2,1,0:T(8,128)(2,1)} fusion(bf16[1,2048,512]{2,1,0:T(8,128)(2,1)} %param.16, bf16[1,512,2048]{2,1,0:T(8,128)(2,1)S(1)} %copy-done, bf16[64,8,2048]{2,1,0:T(8,128)(2,1)} %all-to-all-done.2, f32[512,512]{1,0:T(8,128)S(1)} %fusion.9), kind=kOutput, calls=%fused_computation.7 | convolution fusion | flops 2151153664 | bytes 9437184 | tf_op jit(solution)/shard_map/dot_general | solution.py:19
  191.9 6.1 %all-to-all-start.3 = ((bf16[64,8,2048]{2,1,0:T(8,128)(2,1)}), bf16[64,8,2048]{2,1,0:T(8,128)(2,1)}, u32[]{:S(2)}, u32[]{:S(2)}) async-start(bf16[64,8,2048]{2,1,0:T(8,128)(2,1)} %fusion.1), calls=%async_computation.4 | async-start | bytes 4194304 | tf_op jit(solution)/shard_map/all_to_all | solution.py:62
  198.6 2.6 fusion
  201.2 52.2 %all-to-all-done.3 = bf16[64,8,2048]{2,1,0:T(8,128)(2,1)} async-done(((bf16[64,8,2048]{2,1,0:T(8,128)(2,1)}), bf16[64,8,2048]{2,1,0:T(8,128)(2,1)}, u32[]{:S(2)}, u32[]{:S(2)}) %all-to-all-start.3) | async-done | bytes 2097184 | tf_op jit(solution)/shard_map/all_to_all | solution.py:62
  253.4 5.8 %all-to-all-start.1 = ((bf16[64,8,2048]{2,1,0:T(8,128)(2,1)}), bf16[64,8,2048]{2,1,0:T(8,128)(2,1)}, u32[]{:S(2)}, u32[]{:S(2)}) async-start(bf16[64,8,2048]{2,1,0:T(8,128)(2,1)} %fusion), calls=%async_computation.1 | async-start | bytes 4194304 | tf_op jit(solution)/shard_map/all_to_all | solution.py:59
  259.4 3.4 fusion.60
  262.9 4.2 %gather_fusion.1 = bf16[256,2048]{1,0:T(8,128)(2,1)S(1)} fusion(bf16[512,2048]{1,0:T(8,128)(2,1)} %bitcast.14, s32[1024]{0:T(1024)S(1)} %pad_clamp_fusion), kind=kCustom, calls=%fused_computation.1.clone | custom fusion | bytes 2098176 | tf_op jit(solution)/shard_map/jit(_take)/gather | solution.py:72
  267.1 51.7 %all-gather.9.cloned.1.call-done = bf16[512,2048]{0,1:T(8,128)(2,1)} async-done(((bf16[512,32]{0,1:T(8,128)(2,1)}), bf16[512,2048]{0,1:T(8,128)(2,1)}) %all-gather.9.cloned.1.call-update) | async-done | bytes 2097168 | tf_op jit(solution)/shard_map/all_gather | solution.py:31
  318.8 5.2 %fusion.3 = bf16[256,2048]{1,0:T(8,128)(2,1)} fusion(bf16[2048,512]{1,0:T(8,128)(2,1)} %all-gather.7.cloned.1.call-done, bf16[256,2048]{1,0:T(8,128)(2,1)S(1)} %gather_fusion.1, f32[256]{0:T(256)S(1)} %copy-done.4, pred[256]{0:T(512)(128)(4,1)S(1)} %get-tuple-element.3, bf16[256,2048]{1,0:T(8,128)(2,1)} %all-gather.11.cloned.1.call-done, ...), kind=kOutput, calls=%fused_computation.11 | convolution fusion | flops 1077673984 | bytes 7865600 | tf_op jit(solution)/shard_map/dot_general | solution.py:19
  324.1 4.2 %gather_fusion = bf16[256,2048]{1,0:T(8,128)(2,1)S(1)} fusion(bf16[512,2048]{1,0:T(8,128)(2,1)} %bitcast.10, s32[1024]{0:T(1024)S(1)} %pad_clamp_fusion), kind=kCustom, calls=%fused_computation.clone | custom fusion | bytes 2098176 | tf_op jit(solution)/shard_map/jit(_take)/gather | solution.py:71
  328.4 3.5 fusion.2
  331.9 27.8 %reduce-scatter.5.cloned.1.call-done = bf16[256,256]{1,0:T(8,128)(2,1)} async-done(((bf16[256,2048]{1,0:T(8,128)(2,1)}), bf16[256,256]{1,0:T(8,128)(2,1)}) %reduce-scatter.5.cloned.1.call-update) | async-done | bytes 131088 | tf_op jit(solution)/shard_map/reduce_scatter | solution.py:81
  359.7 1.6 add_convert_fusion
  361.3 41.4 %reduce-scatter.3.cloned.1.call-done = bf16[256,256]{1,0:T(8,128)(2,1)} async-done(((bf16[256,2048]{1,0:T(8,128)(2,1)}), bf16[256,256]{1,0:T(8,128)(2,1)}) %reduce-scatter.3.cloned.1.call-update) | async-done | bytes 131088 | tf_op jit(solution)/shard_map/reduce_scatter | solution.py:75
  402.7 1.6 add_convert_fusion.1
  (33 shorter events, 5.8 us)
Async XLA Ops:
  8.0 177.8 %copy-start = (bf16[1,512,2048]{2,1,0:T(8,128)(2,1)S(1)}, bf16[1,512,2048]{2,1,0:T(8,128)(2,1)}, u32[]{:S(2)}) copy-start(bf16[1,512,2048]{2,1,0:T(8,128)(2,1)} %param.17) | copy-start | bytes 6291460
  8.0 47.1 %all-gather.5.cloned.1.call-start = ((), (), s32[]{:S(2)}) async-start(), calls=%async_computation.6 | async-start | bytes 1179648 | tf_op jit(solution)/shard_map/all_gather | solution.py:26
  59.5 66.0 %all-to-all-start = ((bf16[64,8,2048]{2,1,0:T(8,128)(2,1)}), bf16[64,8,2048]{2,1,0:T(8,128)(2,1)}, u32[]{:S(2)}, u32[]{:S(2)}) async-start(bf16[64,8,2048]{2,1,0:T(8,128)(2,1)} %bitcast.62), calls=%async_computation | async-start | bytes 4194304 | tf_op jit(solution)/shard_map/all_to_all | solution.py:48
  74.3 41.1 %all-gather.11.cloned.1.call-start = ((), (), s32[]{:S(2)}) async-start(), calls=%async_computation.10 | async-start | bytes 1179648 | tf_op jit(solution)/shard_map/all_gather | solution.py:27
  125.5 60.3 %all-to-all-start.2 = ((bf16[64,8,2048]{2,1,0:T(8,128)(2,1)}), bf16[64,8,2048]{2,1,0:T(8,128)(2,1)}, u32[]{:S(2)}, u32[]{:S(2)}) async-start(bf16[64,8,2048]{2,1,0:T(8,128)(2,1)} %bitcast.61), calls=%async_computation.3 | async-start | bytes 4194304 | tf_op jit(solution)/shard_map/all_to_all | solution.py:49
  133.5 125.9 %all-gather.7.cloned.1.call-start = ((), (), s32[]{:S(2)}) async-start(), calls=%async_computation.7 | async-start | bytes 2129920 | tf_op jit(solution)/shard_map/all_gather | solution.py:30
  191.9 61.5 %all-to-all-start.3 = ((bf16[64,8,2048]{2,1,0:T(8,128)(2,1)}), bf16[64,8,2048]{2,1,0:T(8,128)(2,1)}, u32[]{:S(2)}, u32[]{:S(2)}) async-start(bf16[64,8,2048]{2,1,0:T(8,128)(2,1)} %fusion.1), calls=%async_computation.4 | async-start | bytes 4194304 | tf_op jit(solution)/shard_map/all_to_all | solution.py:62
  198.0 120.8 %all-gather.9.cloned.1.call-start = ((), (), s32[]{:S(2)}) async-start(), calls=%async_computation.8 | async-start | bytes 2129920 | tf_op jit(solution)/shard_map/all_gather | solution.py:31
  201.2 58.1 %copy-start.3 = (s32[256,1]{0,1:T(1,128)S(1)}, s32[256,1]{0,1:T(1,128)}, u32[]{:S(2)}) copy-start(s32[256,1]{0,1:T(1,128)} %param.13) | copy-start | bytes 3076
  253.4 70.7 %all-to-all-start.1 = ((bf16[64,8,2048]{2,1,0:T(8,128)(2,1)}), bf16[64,8,2048]{2,1,0:T(8,128)(2,1)}, u32[]{:S(2)}, u32[]{:S(2)}) async-start(bf16[64,8,2048]{2,1,0:T(8,128)(2,1)} %fusion), calls=%async_computation.1 | async-start | bytes 4194304 | tf_op jit(solution)/shard_map/all_to_all | solution.py:59
  259.3 100.5 %reduce-scatter.5.cloned.1.call-start = ((), (), s32[]{:S(2)}) async-start(), calls=%async_computation.11 | async-start | bytes 1179648 | tf_op jit(solution)/shard_map/reduce_scatter | solution.py:81
  262.9 56.0 %copy-start.4 = (f32[256]{0:T(256)S(1)}, f32[256]{0:T(256)}, u32[]{:S(2)}) copy-start(f32[256]{0:T(256)} %param.12) | copy-start | bytes 3076
  324.1 78.7 %reduce-scatter.3.cloned.1.call-start = ((), (), s32[]{:S(2)}) async-start(), calls=%async_computation.9 | async-start | bytes 1179648 | tf_op jit(solution)/shard_map/reduce_scatter | solution.py:75
  328.3 31.4 %copy-start.1 = (bf16[256,256]{1,0:T(8,128)(2,1)S(1)}, bf16[256,256]{1,0:T(8,128)(2,1)}, u32[]{:S(2)}) copy-start(bf16[256,256]{1,0:T(8,128)(2,1)} %param.11) | copy-start | bytes 393220
  328.4 74.4 %copy-start.2 = (bf16[256,256]{1,0:T(8,128)(2,1)S(1)}, bf16[256,256]{1,0:T(8,128)(2,1)}, u32[]{:S(2)}) copy-start(bf16[256,256]{1,0:T(8,128)(2,1)} %param.10) | copy-start | bytes 393220
Sparse Core Ops, SparseCore 0:
  10.9 44.1 all-gather.4
  77.2 38.1 all-gather.10
  324.2 35.5 reduce-scatter.4
  362.4 40.2 reduce-scatter.2
Sparse Core Ops, SparseCore 1:
  137.3 89.7 all-gather.6
  230.2 88.5 all-gather.8
where the time goes:
time: 416 us; the launch traced here: 411 us
  waiting for transfers between devices  313 us (75%)
  starting transfers between devices  35.2 us (8%)
  matrix products  24.4 us (6%)
  local copies, waits for them, and re-layouts  17.5 us (4%)
  between operations  15.3 us (4%)
  other arithmetic  6 us (1%)
    all_to_all x1, waiting for transfers between devices, body(): lax.all_to_all(part_back.reshape(dims_of), 'outer', split_axis=0, concat_...  52.2 us
    all_gather x1, waiting for transfers between devices, body(): lax.all_gather(dense_out, 'outer', axis=1, tiled=True)  51.7 us
    all_to_all x1, waiting for transfers between devices, body(): lax.all_to_all(send_c, 'outer', split_axis=0, concat_axis=0, tiled=True)  48.2 us
    all_gather x1, waiting for transfers between devices, body(): lax.all_gather(tokens, 'node', axis=1, tiled=True)  43.3 us
    reduce_scatter x1, waiting for transfers between devices, body(): lax.psum_scatter((dense_fwd + weight * routed_out).astype(jnp.bfloat16),...  41.4 us
    all_gather x1, waiting for transfers between devices, body(): lax.all_gather(cotangent, 'node', axis=1, tiled=True)  40.3 us
    reduce_scatter x1, waiting for transfers between devices, body(): lax.psum_scatter((dense_bwd + weight * routed_back).astype(jnp.bfloat16),...  27.8 us
    all_to_all x1, starting transfers between devices, body(): lax.all_to_all(send_x, 'outer', split_axis=0, concat_axis=0, tiled=True)  14.8 us
  transfers between devices with their start and end apart: 10, of which 8 were waited for; matrix products, arithmetic and copies ran while one was open for 10% of the time, Pallas kernels for 0%

commit v1 on v0

v1 whole, which is shorter than its diff:
```python
import jax
import jax.numpy as jnp
from jax import lax
from jax.sharding import PartitionSpec as P


def gelu_value(v):
    return 0.5 * v * (1.0 + lax.erf(v * 0.7071067811865476))


def gelu_prime(v):
    return (
        0.5 * (1.0 + lax.erf(v * 0.7071067811865476))
        + v * jnp.exp(-0.5 * v * v) * 0.3989422804014327
    )


def dot(left, right):
    return jnp.dot(left, right, preferred_element_type=jnp.float32)


def contract_last(left, right):
    return lax.dot_general(
        left, right, (((1,), (1,)), ((), ())), preferred_element_type=jnp.float32
    )


def body(tokens, cotangent, gate, expert_ids, dense_in, dense_out, expert_in, expert_out):
    bf16, f32 = jnp.bfloat16, jnp.float32
    n_node, n_outer = lax.axis_size("node"), lax.axis_size("outer")
    z = lax.axis_index("node").astype(jnp.uint32)
    tok_count, feat = tokens.shape
    experts = n_outer * expert_in.shape[0]
    capacity = max(2, 2 * tok_count // n_outer)
    slots = experts * capacity

    def to_right(a):
        return lax.ppermute(a, "node", [(i, (i + 1) % n_node) for i in range(n_node)])

    def to_left(a):
        return lax.ppermute(a, "node", [(i, (i - 1) % n_node) for i in range(n_node)])

    both = jnp.concatenate([tokens, cotangent], axis=0)
    dense_rows = lax.all_gather(both, "node", axis=1, tiled=True)
    weights = lax.all_gather(
        jnp.stack([dense_in, dense_out.T]), "outer", axis=1, tiled=True
    )

    routed = expert_ids[:, 0]
    labels = jnp.arange(experts, dtype=jnp.int32)
    onehot = (routed[:, None] == labels[None, :]).astype(bf16)
    order = jnp.arange(tok_count, dtype=jnp.int32)
    before = (order[:, None] > order[None, :]).astype(bf16)
    ranks = jnp.sum(dot(before, onehot) * onehot.astype(f32), axis=1).astype(jnp.int32)
    slot_of = routed * capacity + ranks
    place = (jnp.arange(slots, dtype=jnp.int32)[:, None] == slot_of[None, :]).astype(bf16)

    send = dot(place, jnp.concatenate([tokens, cotangent], axis=1)).astype(bf16)
    send = jnp.concatenate(
        [
            send[:, :feat].reshape(n_outer, capacity, feat),
            send[:, feat:].reshape(n_outer, capacity, feat),
        ],
        axis=1,
    )
    own = lax.all_to_all(send, "outer", split_axis=0, concat_axis=0, tiled=True)
    own = jnp.concatenate(
        [own[:, :capacity].reshape(slots, feat), own[:, capacity:].reshape(slots, feat)], axis=0
    )

    w_in, w_out = expert_in[0], expert_out[0]

    zero = jnp.uint32(0)

    def start_of(offset):
        return lax.rem(z + jnp.uint32(offset + n_node), jnp.uint32(n_node)) * jnp.uint32(feat)

    def in_slice(offset):
        return lax.dynamic_slice(w_in, (start_of(offset), zero), (feat, w_in.shape[1]))

    def out_slice(offset):
        return lax.dynamic_slice(w_out, (zero, start_of(offset)), (w_out.shape[0], feat))

    half = n_node // 2
    w_ins = {o: in_slice(o) for o in range(-half + 1, half + 1)}
    w_outs = {o: out_slice(o) for o in range(-half + 1, half + 1)}

    pre = dot(own[:slots], w_ins[0])
    grad = contract_last(own[slots:], w_outs[0])
    from_left = from_right = own
    for step in range(1, half):
        from_left, from_right = to_right(from_left), to_left(from_right)
        pre = pre + dot(from_left[:slots], w_ins[-step])
        grad = grad + contract_last(from_left[slots:], w_outs[-step])
        pre = pre + dot(from_right[:slots], w_ins[step])
        grad = grad + contract_last(from_right[slots:], w_outs[step])
    last_x, last_c = to_right(from_left[:slots]), to_left(from_right[slots:])
    pre = pre + dot(last_x, w_ins[half])
    grad = grad + contract_last(last_c, w_outs[half])

    hidden = gelu_value(pre).astype(bf16)
    dpre = (grad * gelu_prime(pre)).astype(bf16)

    def part_out(offset):
        return dot(hidden, w_outs[offset])

    def part_back(offset):
        return contract_last(dpre, w_ins[offset])

    r_out = to_right(part_out(half).astype(bf16))
    l_back = to_left(part_back(half).astype(bf16))
    r_back = l_out = None
    for step in range(half - 1, 0, -1):
        ro, rb = part_out(step), part_back(step)
        lo, lb = part_out(-step), part_back(-step)
        ro = ro + r_out.astype(f32)
        lb = lb + l_back.astype(f32)
        if r_back is not None:
            rb = rb + r_back.astype(f32)
            lo = lo + l_out.astype(f32)
        right = to_right(jnp.concatenate([ro.astype(bf16), rb.astype(bf16)], axis=0))
        left = to_left(jnp.concatenate([lo.astype(bf16), lb.astype(bf16)], axis=0))
        r_out, r_back = right[:slots], right[slots:]
        l_out, l_back = left[:slots], left[slots:]
    sum_out = part_out(0) + r_out.astype(f32) + l_out.astype(f32)
    sum_back = part_back(0) + r_back.astype(f32) + l_back.astype(f32)
    reply = jnp.concatenate(
        [
            sum_out.astype(bf16).reshape(n_outer, capacity, feat),
            sum_back.astype(bf16).reshape(n_outer, capacity, feat),
        ],
        axis=1,
    )
    reply = lax.all_to_all(reply, "outer", split_axis=0, concat_axis=0, tiled=True)

    dense_x, dense_c = dense_rows[:tok_count], dense_rows[tok_count:]
    weight_in, weight_out = weights[0], weights[1]
    dense_pre = dot(dense_x, weight_in)
    dense_hidden = gelu_value(dense_pre).astype(bf16)
    dense_grad = dot(dense_c, weight_out)
    dense_dpre = (dense_grad * gelu_prime(dense_pre)).astype(bf16)
    dense_sum = lax.psum_scatter(
        jnp.concatenate(
            [
                contract_last(dense_hidden, weight_out).astype(bf16),
                contract_last(dense_dpre, weight_in).astype(bf16),
            ],
            axis=0,
        ),
        "node",
        scatter_dimension=1,
        tiled=True,
    ).astype(f32)

    picked_out = lax.dot_general(
        place,
        reply[:, :capacity].reshape(slots, feat),
        (((0,), (0,)), ((), ())),
        preferred_element_type=f32,
    )
    picked_back = lax.dot_general(
        place,
        reply[:, capacity:].reshape(slots, feat),
        (((0,), (0,)), ((), ())),
        preferred_element_type=f32,
    )
    weight = gate[:, None]
    mixed = tokens.astype(f32) + dense_sum[:tok_count] + weight * picked_out
    input_grad = cotangent.astype(f32) + dense_sum[tok_count:] + weight * picked_back
    return mixed.astype(bf16), input_grad.astype(bf16)


def solution(mesh):
    placed = (
        P("outer", "node"),
        P("outer", "node"),
        P("outer"),
        P("outer", None),
        P("outer", "node"),
        P("node", "outer"),
        P("outer", None, "node"),
        P("outer", "node", None),
    )
    return jax.shard_map(
        body,
        mesh=mesh,
        in_specs=placed,
        out_specs=(P("outer", "node"), P("outer", "node")),
        check_vma=False,
    )
```

time: 416 us -> 271 us (0.65)
  waiting for transfers between devices: 313 us -> 113 us
  starting transfers between devices: 35.2 us -> 69.7 us
  blocking collectives: 0 us -> 28.7 us
  local copies, waits for them, and re-layouts: 17.5 us -> 1.02 us
  matrix products: 24.4 us -> 34 us
    all_gather x4 -> x2, waiting for transfers between devices: 135 us -> 29.8 us  [the longest x1 29.8 us: body(): lax.all_gather(jnp.stack([dense_in, dense_out.T]), 'outer', axis=1, tiled...]
    all_to_all x4 -> x1, waiting for transfers between devices: 106 us -> 16.3 us  [body(): lax.all_to_all(reply, 'outer', split_axis=0, concat_axis=0, tiled=True)]
    reduce_scatter x2 -> x1, waiting for transfers between devices: 69.2 us -> 0.02 us  [body(): lax.psum_scatter(jnp.concatenate([contract_last(dense_hidden, weight_out)...]
    ppermute x0 -> x16, waiting for transfers between devices: none -> 67.2 us  [the longest x8 40 us: to_right(): lax.ppermute(a, 'node', [(i, (i + 1) % n_node) for i in range(n_node)])]
    ppermute x0 -> x16, starting transfers between devices: none -> 61.4 us  [the longest x8 44.5 us: to_left(): lax.ppermute(a, 'node', [(i, (i - 1) % n_node) for i in range(n_node)])]
    all_to_all x0 -> x1, blocking collectives: none -> 28.7 us  [body(): own = lax.all_to_all(send, 'outer', split_axis=0, concat_axis=0, tiled=True)]
    all_to_all x4 -> x1, starting transfers between devices: 34.7 us -> 8.17 us  [body(): lax.all_to_all(reply, 'outer', split_axis=0, concat_axis=0, tiled=True)]
    scatter x2 -> x0, local copies, waits for them, and re-layouts: 8.84 us -> none  [body(): jnp.zeros((expert_count * capacity, width), jnp.bfloat16).at[slot_of]]
  transfers between devices with their start and end apart: 10 -> 20, of which waited for: 8 -> 13; matrix products, arithmetic and copies ran while one was open for 10% -> 14% of each run, Pallas kernels for 0% -> 0%
where the time goes in v1:
time: 271 us; the launch traced here: 270 us
  waiting for transfers between devices  113 us (42%)
  starting transfers between devices  69.7 us (26%)
  matrix products  34 us (13%)
  blocking collectives  28.7 us (11%)
  between operations  14.3 us (5%)
  other arithmetic  8.49 us (3%)
    ppermute x8, starting transfers between devices, to_left(): lax.ppermute(a, 'node', [(i, (i - 1) % n_node) for i in range(n_node)])  44.5 us
    ppermute x8, waiting for transfers between devices, to_right(): lax.ppermute(a, 'node', [(i, (i + 1) % n_node) for i in range(n_node)])  40 us
    all_gather x1, waiting for transfers between devices, body(): lax.all_gather(jnp.stack([dense_in, dense_out.T]), 'outer', axis=1, tiled...  29.8 us
    all_to_all x1, blocking collectives, body(): own = lax.all_to_all(send, 'outer', split_axis=0, concat_axis=0, tiled=True)  28.7 us
    ppermute x8, waiting for transfers between devices, to_left(): lax.ppermute(a, 'node', [(i, (i - 1) % n_node) for i in range(n_node)])  27.2 us
    dot_general x18, matrix products, contract_last(): lax.dot_general(left, right, (((1,), (1,)), ((), ())), preferred_element_...  18.4 us
    ppermute x8, starting transfers between devices, to_right(): lax.ppermute(a, 'node', [(i, (i + 1) % n_node) for i in range(n_node)])  16.9 us
    all_to_all x1, waiting for transfers between devices, body(): lax.all_to_all(reply, 'outer', split_axis=0, concat_axis=0, tiled=True)  16.3 us
  transfers between devices with their start and end apart: 20, of which 13 were waited for; matrix products, arithmetic and copies ran while one was open for 14% of the time, Pallas kernels for 0%

profile of v1, /device:TPU:1, one launch (start us, length us, event | category | flops | bytes accessed | tf_op | source)
XLA Modules:
  0.0 269.7 jit_solution(14661831589632640213)
XLA Ops:
  13.6 28.7 %all_to_all.10 = bf16[64,16,256]{2,1,0:T(8,128)(2,1)S(1)} all-to-all(bf16[64,16,256]{2,1,0:T(8,128)(2,1)S(1)} %pad_maximum_fusion.1), channel_id=1, replica_groups=mesh['node'=8,'outer'=64] {'outer'}, dimensions={0} | all-to-all | bytes 1048576 | tf_op jit(solution)/shard_map/all_to_all | solution.py:66
  42.5 10.7 %collective-permute-start.1 = (bf16[1024,256]{1,0:T(8,128)(2,1)S(1)}, bf16[1024,256]{1,0:T(8,128)(2,1)}, u32[]{:S(2)}, u32[]{:S(2)}) collective-permute-start(bf16[1024,256]{1,0:T(8,128)(2,1)S(1)} %pad_maximum_fusion.2), channel_id=1, source_target_pairs={{0,448},{64,0},{128,64},{192,128},{256,192},{320,256},{384,320},{4... | collective-permute-start | bytes 1572872 | tf_op jit(solution)/shard_map/ppermute | solution.py:41
  56.9 15.4 %collective-permute-done.1 = bf16[1024,256]{1,0:T(8,128)(2,1)} collective-permute-done((bf16[1024,256]{1,0:T(8,128)(2,1)S(1)}, bf16[1024,256]{1,0:T(8,128)(2,1)}, u32[]{:S(2)}, u32[]{:S(2)}) %collective-permute-start.1) | collective-permute-done | bytes 524320 | tf_op jit(solution)/shard_map/ppermute | solution.py:41
  72.2 5.4 %collective-permute-start.3 = (bf16[1024,256]{1,0:T(8,128)(2,1)}, bf16[1024,256]{1,0:T(8,128)(2,1)S(1)}, u32[]{:S(2)}, u32[]{:S(2)}) collective-permute-start(bf16[1024,256]{1,0:T(8,128)(2,1)} %collective-permute-done.1), channel_id=1, source_target_pairs={{0,448},{64,0},{128,64},{192,128},{256,192},{320,256},{384,320},{4... | collective-permute-start | bytes 1572872 | tf_op jit(solution)/shard_map/ppermute | solution.py:41
  84.7 8.2 %collective-permute-done.2 = bf16[1024,256]{1,0:T(8,128)(2,1)S(1)} collective-permute-done((bf16[1024,256]{1,0:T(8,128)(2,1)}, bf16[1024,256]{1,0:T(8,128)(2,1)S(1)}, u32[]{:S(2)}, u32[]{:S(2)}) %collective-permute-start.2) | collective-permute-done | bytes 524320 | tf_op jit(solution)/shard_map/ppermute | solution.py:38
  94.8 4.6 %collective-permute-start.5 = (bf16[1024,256]{1,0:T(8,128)(2,1)S(1)}, bf16[1024,256]{1,0:T(8,128)(2,1)S(1)}, u32[]{:S(2)}, u32[]{:S(2)}) collective-permute-start(bf16[1024,256]{1,0:T(8,128)(2,1)S(1)} %collective-permute-done.3), channel_id=1, source_target_pairs={{0,448},{64,0},{128,64},{192,128},{256,192},{320,256},{384,320},{4... | collective-permute-start | bytes 1572872 | tf_op jit(solution)/shard_map/ppermute | solution.py:41
  100.7 6.3 %collective-permute-done.4 = bf16[1024,256]{1,0:T(8,128)(2,1)S(1)} collective-permute-done((bf16[1024,256]{1,0:T(8,128)(2,1)S(1)}, bf16[1024,256]{1,0:T(8,128)(2,1)S(1)}, u32[]{:S(2)}, u32[]{:S(2)}) %collective-permute-start.4) | collective-permute-done | bytes 524320 | tf_op jit(solution)/shard_map/ppermute | solution.py:38
  109.0 4.6 %collective-permute-start.8 = (bf16[512,256]{1,0:T(8,128)(2,1)S(1)}, bf16[512,256]{1,0:T(8,128)(2,1)S(1)}, u32[]{:S(2)}, u32[]{:S(2)}) collective-permute-start(bf16[512,256]{1,0:T(8,128)(2,1)S(1)} %slice.166), channel_id=1, source_target_pairs={{0,448},{64,0},{128,64},{192,128},{256,192},{320,256},{384,320},{4... | collective-permute-start | bytes 786440 | tf_op jit(solution)/shard_map/ppermute | solution.py:41
  119.7 4.6 %collective-permute-start.12 = (bf16[512,256]{1,0:T(8,128)(2,1)S(1)}, bf16[512,256]{1,0:T(8,128)(2,1)S(1)}, u32[]{:S(2)}, u32[]{:S(2)}) collective-permute-start(bf16[512,256]{1,0:T(8,128)(2,1)S(1)} %convolution_convert_fusion.3), channel_id=1, source_target_pairs={{0,448},{64,0},{128,64},{192,128},{256,192},{320,256},{384,320},{4... | collective-permute-start | bytes 786440 | tf_op jit(solution)/shard_map/ppermute | solution.py:41
  128.8 5.0 %collective-permute-start.13 = (bf16[1024,256]{1,0:T(8,128)(2,1)}, bf16[1024,256]{1,0:T(8,128)(2,1)}, u32[]{:S(2)}, u32[]{:S(2)}) collective-permute-start(bf16[1024,256]{1,0:T(8,128)(2,1)} %pad_maximum_fusion.6), channel_id=1, source_target_pairs={{0,448},{64,0},{128,64},{192,128},{256,192},{320,256},{384,320},{4... | collective-permute-start | bytes 1572872 | tf_op jit(solution)/shard_map/ppermute | solution.py:41
  133.8 2.5 collective-permute-done.9
  137.6 29.8 %all-gather.5.cloned.1.call-done = bf16[2,2048,512]{2,1,0:T(8,128)(2,1)} async-done(((bf16[2,32,512]{2,1,0:T(8,128)(2,1)}), bf16[2,2048,512]{2,1,0:T(8,128)(2,1)}) %all-gather.5.cloned.1.call-update) | async-done | bytes 4194320 | tf_op jit(solution)/shard_map/all_gather | solution.py:45
  167.4 3.4 %fusion = f32[256,512]{1,0:T(8,128)} fusion(bf16[2,2048,512]{2,1,0:T(8,128)(2,1)} %all-gather.5.cloned.1.call-done, bf16[512,2048]{1,0:T(8,128)(2,1)} %all-gather.3.cloned.1.call-done), kind=kOutput, calls=%fused_computation.5 | convolution fusion | flops 536870912 | bytes 3670016 | tf_op jit(solution)/shard_map/dot_general | solution.py:19
  170.8 5.1 %convolution_convert_fusion = bf16[256,2048]{1,0:T(8,128)(2,1)} fusion(bf16[2,2048,512]{2,1,0:T(8,128)(2,1)} %all-gather.5.cloned.1.call-done, bf16[512,2048]{1,0:T(8,128)(2,1)} %all-gather.3.cloned.1.call-done, f32[256,512]{1,0:T(8,128)} %fusion), kind=kOutput, calls=%fused_computation | convolution fusion | flops 1075576832 | bytes 6815744 | tf_op jit(solution)/shard_map/dot_general | solution.py:23
  175.9 2.6 convolution_convert_fusion.1
  181.6 3.5 %collective-permute-start.10 = (bf16[1024,256]{1,0:T(8,128)(2,1)S(1)}, bf16[1024,256]{1,0:T(8,128)(2,1)S(1)}, u32[]{:S(2)}, u32[]{:S(2)}) collective-permute-start(bf16[1024,256]{1,0:T(8,128)(2,1)S(1)} %pad_maximum_fusion.4), channel_id=1, source_target_pairs={{0,64},{64,128},{128,192},{192,256},{256,320},{320,384},{384,448},... | collective-permute-start | bytes 1572872 | tf_op jit(solution)/shard_map/ppermute | solution.py:38
  187.7 4.2 %collective-permute-start.14 = (bf16[1024,256]{1,0:T(8,128)(2,1)S(1)}, bf16[1024,256]{1,0:T(8,128)(2,1)S(1)}, u32[]{:S(2)}, u32[]{:S(2)}) collective-permute-start(bf16[1024,256]{1,0:T(8,128)(2,1)S(1)} %pad_maximum_fusion.7), channel_id=1, source_target_pairs={{0,448},{64,0},{128,64},{192,128},{256,192},{320,256},{384,320},{4... | collective-permute-start | bytes 1572872 | tf_op jit(solution)/shard_map/ppermute | solution.py:41
  192.0 10.7 %collective-permute-done.10 = bf16[1024,256]{1,0:T(8,128)(2,1)S(1)} collective-permute-done((bf16[1024,256]{1,0:T(8,128)(2,1)S(1)}, bf16[1024,256]{1,0:T(8,128)(2,1)S(1)}, u32[]{:S(2)}, u32[]{:S(2)}) %collective-permute-start.10) | collective-permute-done | bytes 524320 | tf_op jit(solution)/shard_map/ppermute | solution.py:38
  205.3 6.4 %collective-permute-done.14 = bf16[1024,256]{1,0:T(8,128)(2,1)S(1)} collective-permute-done((bf16[1024,256]{1,0:T(8,128)(2,1)S(1)}, bf16[1024,256]{1,0:T(8,128)(2,1)S(1)}, u32[]{:S(2)}, u32[]{:S(2)}) %collective-permute-start.14) | collective-permute-done | bytes 524320 | tf_op jit(solution)/shard_map/ppermute | solution.py:41
  212.5 5.4 %collective-permute-start.15 = (bf16[1024,256]{1,0:T(8,128)(2,1)S(1)}, bf16[1024,256]{1,0:T(8,128)(2,1)S(1)}, u32[]{:S(2)}, u32[]{:S(2)}) collective-permute-start(bf16[1024,256]{1,0:T(8,128)(2,1)S(1)} %pad_maximum_fusion.8), channel_id=1, source_target_pairs={{0,448},{64,0},{128,64},{192,128},{256,192},{320,256},{384,320},{4... | collective-permute-start | bytes 1572872 | tf_op jit(solution)/shard_map/ppermute | solution.py:41
  217.9 10.9 %collective-permute-done.11 = bf16[1024,256]{1,0:T(8,128)(2,1)S(1)} collective-permute-done((bf16[1024,256]{1,0:T(8,128)(2,1)S(1)}, bf16[1024,256]{1,0:T(8,128)(2,1)S(1)}, u32[]{:S(2)}, u32[]{:S(2)}) %collective-permute-start.11) | collective-permute-done | bytes 524320 | tf_op jit(solution)/shard_map/ppermute | solution.py:38
  228.8 5.3 %collective-permute-done.15 = bf16[1024,256]{1,0:T(8,128)(2,1)S(1)} collective-permute-done((bf16[1024,256]{1,0:T(8,128)(2,1)S(1)}, bf16[1024,256]{1,0:T(8,128)(2,1)S(1)}, u32[]{:S(2)}, u32[]{:S(2)}) %collective-permute-start.15) | collective-permute-done | bytes 524320 | tf_op jit(solution)/shard_map/ppermute | solution.py:41
  235.6 8.2 %all-to-all-start.1 = ((bf16[64,16,256]{2,1,0:T(8,128)(2,1)}), bf16[64,16,256]{2,1,0:T(8,128)(2,1)S(1)}, u32[]{:S(2)}, u32[]{:S(2)}) async-start(bf16[64,16,256]{2,1,0:T(8,128)(2,1)} %pad_maximum_fusion.9), calls=%async_computation.2 | async-start | bytes 1048576 | tf_op jit(solution)/shard_map/all_to_all | solution.py:134
  244.8 16.3 %all-to-all-done.1 = bf16[64,16,256]{2,1,0:T(8,128)(2,1)S(1)} async-done(((bf16[64,16,256]{2,1,0:T(8,128)(2,1)}), bf16[64,16,256]{2,1,0:T(8,128)(2,1)S(1)}, u32[]{:S(2)}, u32[]{:S(2)}) %all-to-all-start.1) | async-done | bytes 524320 | tf_op jit(solution)/shard_map/all_to_all | solution.py:134
  (93 shorter events, 47.6 us)
Async XLA Ops:
  7.2 47.9 %copy-start = (bf16[1,2048,512]{2,1,0:T(8,128)(2,1)S(1)}, bf16[1,2048,512]{2,1,0:T(8,128)(2,1)}, u32[]{:S(2)}) copy-start(bf16[1,2048,512]{2,1,0:T(8,128)(2,1)} %param.14) | copy-start | bytes 6291460
  7.2 130.4 %all-gather.3.cloned.1.call-start = ((), (), s32[]{:S(2)}) async-start(), calls=%async_computation.3 | async-start | bytes 2359296 | tf_op jit(solution)/shard_map/all_gather | solution.py:44
  9.1 158.3 %all-gather.5.cloned.1.call-start = ((), (), s32[]{:S(2)}) async-start(), calls=%async_computation.4 | async-start | bytes 4259840 | tf_op jit(solution)/shard_map/all_gather | solution.py:45
  10.6 233.3 %reduce-scatter.2.cloned.1.call-start = ((), (), s32[]{:S(2)}) async-start(), calls=%async_computation.5 | async-start | bytes 2359296 | tf_op jit(solution)/shard_map/reduce_scatter | solution.py:142
  42.5 29.7 %collective-permute-start.1 = (bf16[1024,256]{1,0:T(8,128)(2,1)S(1)}, bf16[1024,256]{1,0:T(8,128)(2,1)}, u32[]{:S(2)}, u32[]{:S(2)}) collective-permute-start(bf16[1024,256]{1,0:T(8,128)(2,1)S(1)} %pad_maximum_fusion.2), channel_id=1, source_target_pairs={{0,448},{64,0},{128,64},{192,128},{256,192},{320,256},{384,320},{4... | collective-permute-start | bytes 1572872 | tf_op jit(solution)/shard_map/ppermute | solution.py:41
  53.1 24.5 %collective-permute-start = (bf16[1024,256]{1,0:T(8,128)(2,1)S(1)}, bf16[1024,256]{1,0:T(8,128)(2,1)}, u32[]{:S(2)}, u32[]{:S(2)}) collective-permute-start(bf16[1024,256]{1,0:T(8,128)(2,1)S(1)} %pad_maximum_fusion.2), channel_id=1, source_target_pairs={{0,64},{64,128},{128,192},{192,256},{256,320},{320,384},{384,448},... | collective-permute-start | bytes 1572872 | tf_op jit(solution)/shard_map/ppermute | solution.py:38
  72.2 22.6 %collective-permute-start.3 = (bf16[1024,256]{1,0:T(8,128)(2,1)}, bf16[1024,256]{1,0:T(8,128)(2,1)S(1)}, u32[]{:S(2)}, u32[]{:S(2)}) collective-permute-start(bf16[1024,256]{1,0:T(8,128)(2,1)} %collective-permute-done.1), channel_id=1, source_target_pairs={{0,448},{64,0},{128,64},{192,128},{256,192},{320,256},{384,320},{4... | collective-permute-start | bytes 1572872 | tf_op jit(solution)/shard_map/ppermute | solution.py:41
  77.6 15.2 %collective-permute-start.2 = (bf16[1024,256]{1,0:T(8,128)(2,1)}, bf16[1024,256]{1,0:T(8,128)(2,1)S(1)}, u32[]{:S(2)}, u32[]{:S(2)}) collective-permute-start(bf16[1024,256]{1,0:T(8,128)(2,1)} %collective-permute-done), channel_id=1, source_target_pairs={{0,64},{64,128},{128,192},{192,256},{256,320},{320,384},{384,448},... | collective-permute-start | bytes 1572872 | tf_op jit(solution)/shard_map/ppermute | solution.py:38
  92.9 14.1 %collective-permute-start.4 = (bf16[1024,256]{1,0:T(8,128)(2,1)S(1)}, bf16[1024,256]{1,0:T(8,128)(2,1)S(1)}, u32[]{:S(2)}, u32[]{:S(2)}) collective-permute-start(bf16[1024,256]{1,0:T(8,128)(2,1)S(1)} %collective-permute-done.2), channel_id=1, source_target_pairs={{0,64},{64,128},{128,192},{192,256},{256,320},{320,384},{384,448},... | collective-permute-start | bytes 1572872 | tf_op jit(solution)/shard_map/ppermute | solution.py:38
  94.8 14.1 %collective-permute-start.5 = (bf16[1024,256]{1,0:T(8,128)(2,1)S(1)}, bf16[1024,256]{1,0:T(8,128)(2,1)S(1)}, u32[]{:S(2)}, u32[]{:S(2)}) collective-permute-start(bf16[1024,256]{1,0:T(8,128)(2,1)S(1)} %collective-permute-done.3), channel_id=1, source_target_pairs={{0,448},{64,0},{128,64},{192,128},{256,192},{320,256},{384,320},{4... | collective-permute-start | bytes 1572872 | tf_op jit(solution)/shard_map/ppermute | solution.py:41
  107.0 8.3 %collective-permute-start.6 = (bf16[512,256]{1,0:T(8,128)(2,1)S(1)}, bf16[512,256]{1,0:T(8,128)(2,1)S(1)}, u32[]{:S(2)}, u32[]{:S(2)}) collective-permute-start(bf16[512,256]{1,0:T(8,128)(2,1)S(1)} %slice.159), channel_id=1, source_target_pairs={{0,64},{64,128},{128,192},{192,256},{256,320},{320,384},{384,448},... | collective-permute-start | bytes 786440 | tf_op jit(solution)/shard_map/ppermute | solution.py:38
  109.0 9.4 %collective-permute-start.8 = (bf16[512,256]{1,0:T(8,128)(2,1)S(1)}, bf16[512,256]{1,0:T(8,128)(2,1)S(1)}, u32[]{:S(2)}, u32[]{:S(2)}) collective-permute-start(bf16[512,256]{1,0:T(8,128)(2,1)S(1)} %slice.166), channel_id=1, source_target_pairs={{0,448},{64,0},{128,64},{192,128},{256,192},{320,256},{384,320},{4... | collective-permute-start | bytes 786440 | tf_op jit(solution)/shard_map/ppermute | solution.py:41
  116.4 8.5 %collective-permute-start.7 = (bf16[512,256]{1,0:T(8,128)(2,1)S(1)}, bf16[512,256]{1,0:T(8,128)(2,1)S(1)}, u32[]{:S(2)}, u32[]{:S(2)}) collective-permute-start(bf16[512,256]{1,0:T(8,128)(2,1)S(1)} %convolution_convert_fusion.6), channel_id=1, source_target_pairs={{0,64},{64,128},{128,192},{192,256},{256,320},{320,384},{384,448},... | collective-permute-start | bytes 786440 | tf_op jit(solution)/shard_map/ppermute | solution.py:38
  119.7 7.9 %collective-permute-start.12 = (bf16[512,256]{1,0:T(8,128)(2,1)S(1)}, bf16[512,256]{1,0:T(8,128)(2,1)S(1)}, u32[]{:S(2)}, u32[]{:S(2)}) collective-permute-start(bf16[512,256]{1,0:T(8,128)(2,1)S(1)} %convolution_convert_fusion.3), channel_id=1, source_target_pairs={{0,448},{64,0},{128,64},{192,128},{256,192},{320,256},{384,320},{4... | collective-permute-start | bytes 786440 | tf_op jit(solution)/shard_map/ppermute | solution.py:41
  125.3 11.1 %collective-permute-start.9 = (bf16[1024,256]{1,0:T(8,128)(2,1)S(1)}, bf16[1024,256]{1,0:T(8,128)(2,1)S(1)}, u32[]{:S(2)}, u32[]{:S(2)}) collective-permute-start(bf16[1024,256]{1,0:T(8,128)(2,1)S(1)} %pad_maximum_fusion.3), channel_id=1, source_target_pairs={{0,64},{64,128},{128,192},{192,256},{256,320},{320,384},{384,448},... | collective-permute-start | bytes 1572872 | tf_op jit(solution)/shard_map/ppermute | solution.py:38
  128.8 56.3 %collective-permute-start.13 = (bf16[1024,256]{1,0:T(8,128)(2,1)}, bf16[1024,256]{1,0:T(8,128)(2,1)}, u32[]{:S(2)}, u32[]{:S(2)}) collective-permute-start(bf16[1024,256]{1,0:T(8,128)(2,1)} %pad_maximum_fusion.6), channel_id=1, source_target_pairs={{0,448},{64,0},{128,64},{192,128},{256,192},{320,256},{384,320},{4... | collective-permute-start | bytes 1572872 | tf_op jit(solution)/shard_map/ppermute | solution.py:41
  181.6 21.1 %collective-permute-start.10 = (bf16[1024,256]{1,0:T(8,128)(2,1)S(1)}, bf16[1024,256]{1,0:T(8,128)(2,1)S(1)}, u32[]{:S(2)}, u32[]{:S(2)}) collective-permute-start(bf16[1024,256]{1,0:T(8,128)(2,1)S(1)} %pad_maximum_fusion.4), channel_id=1, source_target_pairs={{0,64},{64,128},{128,192},{192,256},{256,320},{320,384},{384,448},... | collective-permute-start | bytes 1572872 | tf_op jit(solution)/shard_map/ppermute | solution.py:38
  187.7 24.1 %collective-permute-start.14 = (bf16[1024,256]{1,0:T(8,128)(2,1)S(1)}, bf16[1024,256]{1,0:T(8,128)(2,1)S(1)}, u32[]{:S(2)}, u32[]{:S(2)}) collective-permute-start(bf16[1024,256]{1,0:T(8,128)(2,1)S(1)} %pad_maximum_fusion.7), channel_id=1, source_target_pairs={{0,448},{64,0},{128,64},{192,128},{256,192},{320,256},{384,320},{4... | collective-permute-start | bytes 1572872 | tf_op jit(solution)/shard_map/ppermute | solution.py:41
  203.4 25.4 %collective-permute-start.11 = (bf16[1024,256]{1,0:T(8,128)(2,1)S(1)}, bf16[1024,256]{1,0:T(8,128)(2,1)S(1)}, u32[]{:S(2)}, u32[]{:S(2)}) collective-permute-start(bf16[1024,256]{1,0:T(8,128)(2,1)S(1)} %pad_maximum_fusion.5), channel_id=1, source_target_pairs={{0,64},{64,128},{128,192},{192,256},{256,320},{320,384},{384,448},... | collective-permute-start | bytes 1572872 | tf_op jit(solution)/shard_map/ppermute | solution.py:38
  212.5 21.6 %collective-permute-start.15 = (bf16[1024,256]{1,0:T(8,128)(2,1)S(1)}, bf16[1024,256]{1,0:T(8,128)(2,1)S(1)}, u32[]{:S(2)}, u32[]{:S(2)}) collective-permute-start(bf16[1024,256]{1,0:T(8,128)(2,1)S(1)} %pad_maximum_fusion.8), channel_id=1, source_target_pairs={{0,448},{64,0},{128,64},{192,128},{256,192},{320,256},{384,320},{4... | collective-permute-start | bytes 1572872 | tf_op jit(solution)/shard_map/ppermute | solution.py:41
  234.4 26.7 %copy-start.5 = (bf16[256,256]{1,0:T(8,128)(2,1)S(1)}, bf16[256,256]{1,0:T(8,128)(2,1)}, u32[]{:S(2)}) copy-start(bf16[256,256]{1,0:T(8,128)(2,1)} %param.9) | copy-start | bytes 393220
  234.4 26.7 %copy-start.7 = (f32[256]{0:T(256)S(1)}, f32[256]{0:T(256)}, u32[]{:S(2)}) copy-start(f32[256]{0:T(256)} %param.10) | copy-start | bytes 3076
  234.8 27.4 %copy-start.6 = (bf16[256,256]{1,0:T(8,128)(2,1)S(1)}, bf16[256,256]{1,0:T(8,128)(2,1)}, u32[]{:S(2)}) copy-start(bf16[256,256]{1,0:T(8,128)(2,1)} %param.8) | copy-start | bytes 393220
  235.6 25.5 %all-to-all-start.1 = ((bf16[64,16,256]{2,1,0:T(8,128)(2,1)}), bf16[64,16,256]{2,1,0:T(8,128)(2,1)S(1)}, u32[]{:S(2)}, u32[]{:S(2)}) async-start(bf16[64,16,256]{2,1,0:T(8,128)(2,1)} %pad_maximum_fusion.9), calls=%async_computation.2 | async-start | bytes 1048576 | tf_op jit(solution)/shard_map/all_to_all | solution.py:134
  (4 other events, 33.9 us)
Sparse Core Ops, SparseCore 0:
  10.0 60.5 all-gather.2
  74.6 92.7 all-gather.4
  180.3 52.2 reduce-scatter.1

commit v2 on v1

v2 whole, which is shorter than its diff:
```python
import jax
import jax.numpy as jnp
from jax import lax
from jax.sharding import PartitionSpec as P


def gelu_value(v):
    return 0.5 * v * (1.0 + lax.erf(v * 0.7071067811865476))


def gelu_prime(v):
    return (
        0.5 * (1.0 + lax.erf(v * 0.7071067811865476))
        + v * jnp.exp(-0.5 * v * v) * 0.3989422804014327
    )


def dot(left, right):
    return jnp.dot(left, right, preferred_element_type=jnp.float32)


def contract_last(left, right):
    return lax.dot_general(
        left, right, (((1,), (1,)), ((), ())), preferred_element_type=jnp.float32
    )


def body(tokens, cotangent, gate, expert_ids, dense_in, dense_out, expert_in, expert_out):
    bf16, f32 = jnp.bfloat16, jnp.float32
    n_node, n_outer = lax.axis_size("node"), lax.axis_size("outer")
    z = lax.axis_index("node").astype(jnp.uint32)
    tok_count, feat = tokens.shape
    experts = n_outer * expert_in.shape[0]
    capacity = max(2, 2 * tok_count // n_outer)
    slots = experts * capacity

    def to_right(a):
        return lax.ppermute(a, "node", [(i, (i + 1) % n_node) for i in range(n_node)])

    def to_left(a):
        return lax.ppermute(a, "node", [(i, (i - 1) % n_node) for i in range(n_node)])

    zero = jnp.uint32(0)
    dense_right = to_right(jnp.concatenate([tokens, cotangent], axis=0))
    dense_left = to_left(jnp.concatenate([cotangent, tokens], axis=0))

    routed = expert_ids[:, 0]
    labels = jnp.arange(experts, dtype=jnp.int32)
    onehot = (routed[:, None] == labels[None, :]).astype(bf16)
    order = jnp.arange(tok_count, dtype=jnp.int32)
    before = (order[:, None] > order[None, :]).astype(bf16)
    ranks = jnp.sum(dot(before, onehot) * onehot.astype(f32), axis=1).astype(jnp.int32)
    slot_of = routed * capacity + ranks
    place = (jnp.arange(slots, dtype=jnp.int32)[:, None] == slot_of[None, :]).astype(bf16)

    send = dot(place, jnp.concatenate([tokens, cotangent], axis=1)).astype(bf16)
    send = jnp.concatenate(
        [
            send[:, :feat].reshape(n_outer, capacity, feat),
            send[:, feat:].reshape(n_outer, capacity, feat),
        ],
        axis=1,
    )
    own = lax.all_to_all(send, "outer", split_axis=0, concat_axis=0, tiled=True)
    own = jnp.concatenate(
        [own[:, :capacity].reshape(slots, feat), own[:, capacity:].reshape(slots, feat)], axis=0
    )
    own, dense_right, dense_left = lax.optimization_barrier((own, dense_right, dense_left))
    rows = lax.all_gather(own, "node", axis=1, tiled=True)

    depth, width = dense_in.shape
    pieces = jnp.concatenate([dense_in, dense_out.T], axis=0)
    pieces = jnp.stack([pieces[:, : width // 2], pieces[:, width // 2 :]])
    pieces, own = lax.optimization_barrier((pieces, own))
    pieces = jnp.broadcast_to(pieces, (n_outer // 2,) + pieces.shape)
    near = lax.all_to_all(
        pieces.reshape(n_outer, 2 * depth, width // 2),
        "outer",
        split_axis=0,
        concat_axis=0,
        tiled=True,
    )

    def dense_up(half_weights):
        w_i = half_weights[:, :depth].reshape(n_outer * depth, width // 2)
        w_o = half_weights[:, depth:].reshape(n_outer * depth, width // 2)
        pre_d = dot(dense_rows[:tok_count], w_i)
        grad_d = dot(dense_rows[tok_count:], w_o)
        return (
            w_i,
            w_o,
            gelu_value(pre_d).astype(bf16),
            (grad_d * gelu_prime(pre_d)).astype(bf16),
        )

    def start_of(offset):
        return lax.rem(z + jnp.uint32(offset + n_node), jnp.uint32(n_node)) * jnp.uint32(feat)

    half = n_node // 2
    dense_rows = jnp.zeros((2 * tok_count, n_node * feat), bf16)

    def put(array, values, offset, row):
        return lax.dynamic_update_slice(array, values, (jnp.uint32(row), start_of(offset)))

    def put_pair(array, from_left, from_right, hop):
        array = put(array, from_left, -hop, 0)
        array = put(array, from_right[:tok_count], hop, tok_count)
        return put(array, from_right[tok_count:], hop, 0)

    dense_rows = put(dense_rows, tokens, 0, 0)
    dense_rows = put(dense_rows, cotangent, 0, tok_count)
    dense_rows = put_pair(dense_rows, dense_right, dense_left, 1)
    dense_right, dense_left = to_right(dense_right), to_left(dense_left)
    for hop in range(2, half):
        dense_rows = put_pair(dense_rows, dense_right, dense_left, hop)
        if hop == half - 1:
            dense_right, dense_left = dense_right[:tok_count], dense_left[:tok_count]
        dense_right, dense_left = to_right(dense_right), to_left(dense_left)
    dense_rows = put(dense_rows, dense_right, half, 0)
    dense_rows = put(dense_rows, dense_left, half, tok_count)

    far = lax.ppermute(near, "outer", [(i, i ^ 1) for i in range(n_outer)])
    dense = dense_up(near)
    rows, dense = lax.optimization_barrier((rows, dense))
    w_in, w_out = expert_in[0], expert_out[0]
    pre = dot(rows[:slots], w_in)
    grad = contract_last(rows[slots:], w_out)
    back = contract_last((grad * gelu_prime(pre)).astype(bf16), w_in).astype(bf16)
    hidden = gelu_value(pre).astype(bf16)

    def part_out(offset):
        weights = lax.dynamic_slice(w_out, (zero, start_of(offset)), (w_out.shape[0], feat))
        return dot(hidden, weights)

    mid = slots // 2
    first = part_out(half).astype(bf16)
    back, first, far, dense_rows = lax.optimization_barrier((back, first, far, dense_rows))
    sum_back = lax.psum_scatter(back, "node", scatter_dimension=1, tiled=True)
    right, left = to_right(first[:mid]), to_left(first[mid:])
    for step in range(half - 1, 0, -1):
        ro, lo = part_out(step), part_out(-step)
        if step == half - 1:
            ro = jnp.concatenate([ro[:mid] + right.astype(f32), ro[mid:]], axis=0)
            lo = jnp.concatenate([lo[:mid], lo[mid:] + left.astype(f32)], axis=0)
        else:
            ro, lo = ro + right.astype(f32), lo + left.astype(f32)
        right, left = ro.astype(bf16), lo.astype(bf16)
        if step == half - 1:
            wi_n, wo_n, hid_n, dpre_n = dense
            wi_f, wo_f, hid_f, dpre_f = dense_up(far)
            right, left, hid_f, dpre_f = lax.optimization_barrier((right, left, hid_f, dpre_f))
        elif step == half - 2:
            dense = jnp.concatenate(
                [
                    contract_last(hid_n, wo_n) + contract_last(hid_f, wo_f),
                    contract_last(dpre_n, wi_n) + contract_last(dpre_f, wi_f),
                ],
                axis=0,
            ).astype(bf16)
            right, left, dense = lax.optimization_barrier((right, left, dense))
        right, left = to_right(right), to_left(left)
    sum_out = (part_out(0) + right.astype(f32) + left.astype(f32)).astype(bf16)
    dense_sum = lax.psum_scatter(dense, "node", scatter_dimension=1, tiled=True).astype(f32)

    reply = jnp.concatenate(
        [
            sum_out.reshape(n_outer, capacity, feat),
            sum_back.reshape(n_outer, capacity, feat),
        ],
        axis=1,
    )
    reply = lax.all_to_all(reply, "outer", split_axis=0, concat_axis=0, tiled=True)

    picked_out = lax.dot_general(
        place,
        reply[:, :capacity].reshape(slots, feat),
        (((0,), (0,)), ((), ())),
        preferred_element_type=f32,
    )
    picked_back = lax.dot_general(
        place,
        reply[:, capacity:].reshape(slots, feat),
        (((0,), (0,)), ((), ())),
        preferred_element_type=f32,
    )
    scale = gate[:, None]
    mixed = tokens.astype(f32) + dense_sum[:tok_count] + scale * picked_out
    input_grad = cotangent.astype(f32) + dense_sum[tok_count:] + scale * picked_back
    return mixed.astype(bf16), input_grad.astype(bf16)


def solution(mesh):
    placed = (
        P("outer", "node"),
        P("outer", "node"),
        P("outer"),
        P("outer", None),
        P("outer", "node"),
        P("node", "outer"),
        P("outer", None, "node"),
        P("outer", "node", None),
    )
    return jax.shard_map(
        body,
        mesh=mesh,
        in_specs=placed,
        out_specs=(P("outer", "node"), P("outer", "node")),
        check_vma=False,
    )
```

time: 271 us -> 238 us (0.88); the launches traced: 270 us -> 233 us
  waiting for transfers between devices: 113 us -> 58.7 us
  starting transfers between devices: 69.7 us -> 103 us
  blocking collectives: 28.7 us -> 0 us
  local copies, waits for them, and re-layouts: 1.02 us -> 21.4 us
  matrix products: 34 us -> 28.2 us
    all_to_all x1 -> x0, blocking collectives: 28.7 us -> none  [body(): own = lax.all_to_all(send, 'outer', split_axis=0, concat_axis=0, tiled=True)]
    all_gather x2 -> x1, waiting for transfers between devices: 29.8 us -> 3.78 us  [body(): rows = lax.all_gather(own, 'node', axis=1, tiled=True)]
    all_to_all x0 -> x2, starting transfers between devices: none -> 22.9 us  [the longest x1 11.8 us: body(): own = lax.all_to_all(send, 'outer', split_axis=0, concat_axis=0, tiled=True)]
    ppermute x8, waiting for transfers between devices: 40 us -> 22.7 us  [to_right(): lax.ppermute(a, 'node', [(i, (i + 1) % n_node) for i in range(n_node)])]
    reduce_scatter x1 -> x2, waiting for transfers between devices: 0.02 us -> 16.9 us  [the longest x1 16.8 us: body(): lax.psum_scatter(dense, 'node', scatter_dimension=1, tiled=True).astype(f32)]
    ppermute x8, waiting for transfers between devices: 27.2 us -> 10.7 us  [to_left(): lax.ppermute(a, 'node', [(i, (i - 1) % n_node) for i in range(n_node)])]
    all_to_all x1, waiting for transfers between devices: 16.3 us -> 0.01 us  [body(): lax.all_to_all(reply, 'outer', split_axis=0, concat_axis=0, tiled=True)]
    dynamic_update_slice x0 -> x12, local copies, waits for them, and re-layouts: none -> 11.1 us  [put(): lax.dynamic_update_slice(array, values, (jnp.uint32(row), start_of(offset)))]
  transfers between devices with their start and end apart: 20 -> 23, of which waited for: 13 -> 12; matrix products, arithmetic and copies ran while one was open for 14% -> 21% of each run, Pallas kernels for 0% -> 0%
where the time goes in v2:
time: 238 us; the launch traced here: 233 us
  starting transfers between devices  103 us (43%)
  waiting for transfers between devices  58.7 us (25%)
  matrix products  28.2 us (12%)
  local copies, waits for them, and re-layouts  21.4 us (9%)
  between operations  14.3 us (6%)
  other arithmetic  7.7 us (3%)
    ppermute x8, starting transfers between devices, to_left(): lax.ppermute(a, 'node', [(i, (i - 1) % n_node) for i in range(n_node)])  41.2 us
    ppermute x8, waiting for transfers between devices, to_right(): lax.ppermute(a, 'node', [(i, (i + 1) % n_node) for i in range(n_node)])  22.7 us
    ppermute x8, starting transfers between devices, to_right(): lax.ppermute(a, 'node', [(i, (i + 1) % n_node) for i in range(n_node)])  19.5 us
    dot_general x15, matrix products, dot(): return jnp.dot(left, right, preferred_element_type=jnp.float32)  17.7 us
    reduce_scatter x1, waiting for transfers between devices, body(): lax.psum_scatter(dense, 'node', scatter_dimension=1, tiled=True).astype(f32)  16.8 us
    all_to_all x1, starting transfers between devices, body(): lax.all_to_all(reply, 'outer', split_axis=0, concat_axis=0, tiled=True)  14.9 us
    all_to_all x1, starting transfers between devices, body(): own = lax.all_to_all(send, 'outer', split_axis=0, concat_axis=0, tiled=True)  11.8 us
    all_to_all x1, starting transfers between devices, body(): lax.all_to_all(pieces.reshape(n_outer, 2 * depth, width // 2), 'outer', s...  11.1 us
  transfers between devices with their start and end apart: 23, of which 12 were waited for; matrix products, arithmetic and copies ran while one was open for 21% of the time, Pallas kernels for 0%

profile of v2, /device:TPU:1, one launch (start us, length us, event | category | flops | bytes accessed | tf_op | source)
XLA Modules:
  0.0 232.8 jit_solution(39463395833618201)
XLA Ops:
  11.1 11.8 %all-to-all-start = ((bf16[64,16,256]{2,1,0:T(8,128)(2,1)}), bf16[64,16,256]{2,1,0:T(8,128)(2,1)S(1)}, u32[]{:S(2)}, u32[]{:S(2)}) async-start(bf16[64,16,256]{2,1,0:T(8,128)(2,1)} %pad_maximum_fusion.1), calls=%async_computation | async-start | bytes 1048576 | tf_op jit(solution)/shard_map/all_to_all | solution.py:64
  23.0 4.0 %collective-permute-start = (bf16[512,256]{1,0:T(8,128)(2,1)S(1)}, bf16[512,256]{1,0:T(8,128)(2,1)}, u32[]{:S(2)}, u32[]{:S(2)}) collective-permute-start(bf16[512,256]{1,0:T(8,128)(2,1)S(1)} %get-tuple-element.55), channel_id=1, source_target_pairs={{0,64},{64,128},{128,192},{192,256},{256,320},{320,384},{384,448},... | collective-permute-start | bytes 786440 | tf_op jit(solution)/shard_map/ppermute | solution.py:38
  27.0 8.6 %collective-permute-start.1 = (bf16[512,256]{1,0:T(8,128)(2,1)S(1)}, bf16[512,256]{1,0:T(8,128)(2,1)}, u32[]{:S(2)}, u32[]{:S(2)}) collective-permute-start(bf16[512,256]{1,0:T(8,128)(2,1)S(1)} %get-tuple-element.54), channel_id=1, source_target_pairs={{0,448},{64,0},{128,64},{192,128},{256,192},{320,256},{384,320},{4... | collective-permute-start | bytes 786440 | tf_op jit(solution)/shard_map/ppermute | solution.py:41
  35.6 4.6 %all-to-all-done = bf16[64,16,256]{2,1,0:T(8,128)(2,1)S(1)} async-done(((bf16[64,16,256]{2,1,0:T(8,128)(2,1)}), bf16[64,16,256]{2,1,0:T(8,128)(2,1)S(1)}, u32[]{:S(2)}, u32[]{:S(2)}) %all-to-all-start) | async-done | bytes 524320 | tf_op jit(solution)/shard_map/all_to_all | solution.py:64
  42.8 11.1 %all-to-all-start.1 = ((bf16[64,64,256]{2,1,0:T(8,128)(2,1)}), bf16[64,64,256]{2,1,0:T(8,128)(2,1)}, u32[]{:S(2)}, u32[]{:S(2)}) async-start(bf16[64,64,256]{2,1,0:T(8,128)(2,1)} %bitcast.92), calls=%async_computation.1 | async-start | bytes 4194304 | tf_op jit(solution)/shard_map/all_to_all | solution.py:76
  57.0 6.0 %collective-permute-start.3 = (bf16[512,256]{1,0:T(8,128)(2,1)}, bf16[512,256]{1,0:T(8,128)(2,1)S(1)}, u32[]{:S(2)}, u32[]{:S(2)}) collective-permute-start(bf16[512,256]{1,0:T(8,128)(2,1)} %collective-permute-done.1), channel_id=1, source_target_pairs={{0,448},{64,0},{128,64},{192,128},{256,192},{320,256},{384,320},{4... | collective-permute-start | bytes 786440 | tf_op jit(solution)/shard_map/ppermute | solution.py:41
  70.4 5.3 %collective-permute-start.5 = (bf16[512,256]{1,0:T(8,128)(2,1)S(1)}, bf16[512,256]{1,0:T(8,128)(2,1)S(1)}, u32[]{:S(2)}, u32[]{:S(2)}) collective-permute-start(bf16[512,256]{1,0:T(8,128)(2,1)S(1)} %collective-permute-done.3), channel_id=1, source_target_pairs={{0,448},{64,0},{128,64},{192,128},{256,192},{320,256},{384,320},{4... | collective-permute-start | bytes 786440 | tf_op jit(solution)/shard_map/ppermute | solution.py:41
  75.7 3.1 %collective-permute-done.2 = bf16[512,256]{1,0:T(8,128)(2,1)S(1)} collective-permute-done((bf16[512,256]{1,0:T(8,128)(2,1)}, bf16[512,256]{1,0:T(8,128)(2,1)S(1)}, u32[]{:S(2)}, u32[]{:S(2)}) %collective-permute-start.2) | collective-permute-done | bytes 262176 | tf_op jit(solution)/shard_map/ppermute | solution.py:38
  82.8 9.2 %collective-permute-done.4 = bf16[512,256]{1,0:T(8,128)(2,1)S(1)} collective-permute-done((bf16[512,256]{1,0:T(8,128)(2,1)S(1)}, bf16[512,256]{1,0:T(8,128)(2,1)S(1)}, u32[]{:S(2)}, u32[]{:S(2)}) %collective-permute-start.4) | collective-permute-done | bytes 262176 | tf_op jit(solution)/shard_map/ppermute | solution.py:38
  95.4 4.6 %collective-permute-start.7 = (bf16[256,256]{1,0:T(8,128)(2,1)S(1)}, bf16[256,256]{1,0:T(8,128)(2,1)S(1)}, u32[]{:S(2)}, u32[]{:S(2)}) collective-permute-start(bf16[256,256]{1,0:T(8,128)(2,1)S(1)} %get-tuple-element.52), channel_id=1, source_target_pairs={{0,448},{64,0},{128,64},{192,128},{256,192},{320,256},{384,320},{4... | collective-permute-start | bytes 393224 | tf_op jit(solution)/shard_map/ppermute | solution.py:41
  105.3 3.9 %collective-permute-start.8 = (bf16[64,64,256]{2,1,0:T(8,128)(2,1)}, bf16[64,64,256]{2,1,0:T(8,128)(2,1)}, u32[]{:S(2)}, u32[]{:S(2)}) collective-permute-start(bf16[64,64,256]{2,1,0:T(8,128)(2,1)} %all-to-all-done.1), channel_id=1, source_target_pairs={{0,1},{1,0},{2,3},{3,2},{4,5},{5,4},{6,7},{7,6},{8,9},{9,8},{10,11... | collective-permute-start | bytes 6291464 | tf_op jit(solution)/shard_map/ppermute | solution.py:122
  115.3 3.8 %all-gather.2.cloned.1.call-done = bf16[1024,2048]{1,0:T(8,128)(2,1)} async-done(((bf16[1024,256]{1,0:T(8,128)(2,1)}), bf16[1024,2048]{1,0:T(8,128)(2,1)}) %all-gather.2.cloned.1.call-update) | async-done | bytes 4194320 | tf_op jit(solution)/shard_map/all_gather | solution.py:69
  119.1 4.5 %multiply_convert_fusion = (bf16[512,512]{1,0:T(8,128)(2,1)S(1)}, f32[512,512]{1,0:T(8,128)}) fusion(bf16[1,2048,512]{2,1,0:T(8,128)(2,1)} %param.14, bf16[1024,2048]{1,0:T(8,128)(2,1)} %all-gather.2.cloned.1.call-done), kind=kOutput, calls=%fused_computation.40 | convolution fusion | flops 1075052544 | bytes 5767168 | tf_op jit(solution)/shard_map/dot_general | solution.py:19
  123.9 6.5 %convolution_convert_fusion = bf16[512,2048]{1,0:T(8,128)(2,1)} fusion(bf16[1,2048,512]{2,1,0:T(8,128)(2,1)} %param.14, bf16[1,512,2048]{2,1,0:T(8,128)(2,1)S(1)} %copy-done, bf16[1024,2048]{1,0:T(8,128)(2,1)} %all-gather.2.cloned.1.call-done, f32[512,512]{1,0:T(8,128)} %get-tuple-element.61), kind=kOutput, calls=%fused_computation | convolution fusion | flops 2151153664 | bytes 9437184 | tf_op jit(solution)/shard_map/dot_general | solution.py:23
  130.9 3.5 %collective-permute-start.9 = (bf16[256,256]{1,0:T(8,128)(2,1)S(1)}, bf16[256,256]{1,0:T(8,128)(2,1)S(1)}, u32[]{:S(2)}, u32[]{:S(2)}) collective-permute-start(bf16[256,256]{1,0:T(8,128)(2,1)S(1)} %get-tuple-element.51), channel_id=1, source_target_pairs={{0,64},{64,128},{128,192},{192,256},{256,320},{320,384},{384,448},... | collective-permute-start | bytes 393224 | tf_op jit(solution)/shard_map/ppermute | solution.py:38
  134.3 3.0 %collective-permute-start.10 = (bf16[256,256]{1,0:T(8,128)(2,1)S(1)}, bf16[256,256]{1,0:T(8,128)(2,1)S(1)}, u32[]{:S(2)}, u32[]{:S(2)}) collective-permute-start(bf16[256,256]{1,0:T(8,128)(2,1)S(1)} %get-tuple-element.50), channel_id=1, source_target_pairs={{0,448},{64,0},{128,64},{192,128},{256,192},{320,256},{384,320},{4... | collective-permute-start | bytes 393224 | tf_op jit(solution)/shard_map/ppermute | solution.py:41
  147.7 4.4 %collective-permute-start.12 = (bf16[512,256]{1,0:T(8,128)(2,1)}, bf16[512,256]{1,0:T(8,128)(2,1)S(1)}, u32[]{:S(2)}, u32[]{:S(2)}) collective-permute-start(bf16[512,256]{1,0:T(8,128)(2,1)} %pad_maximum_fusion.7), channel_id=1, source_target_pairs={{0,448},{64,0},{128,64},{192,128},{256,192},{320,256},{384,320},{4... | collective-permute-start | bytes 786440 | tf_op jit(solution)/shard_map/ppermute | solution.py:41
  154.6 5.8 %collective-permute-done.11 = bf16[512,256]{1,0:T(8,128)(2,1)} collective-permute-done((bf16[512,256]{1,0:T(8,128)(2,1)S(1)}, bf16[512,256]{1,0:T(8,128)(2,1)}, u32[]{:S(2)}, u32[]{:S(2)}) %collective-permute-start.11) | collective-permute-done | bytes 262176 | tf_op jit(solution)/shard_map/ppermute | solution.py:38
  163.7 4.1 %collective-permute-start.15 = (bf16[512,256]{1,0:T(8,128)(2,1)S(1)}, bf16[512,256]{1,0:T(8,128)(2,1)S(1)}, u32[]{:S(2)}, u32[]{:S(2)}) collective-permute-start(bf16[512,256]{1,0:T(8,128)(2,1)S(1)} %copy-done.7), channel_id=1, source_target_pairs={{0,448},{64,0},{128,64},{192,128},{256,192},{320,256},{384,320},{4... | collective-permute-start | bytes 786440 | tf_op jit(solution)/shard_map/ppermute | solution.py:41
  170.3 5.6 %collective-permute-done.15 = bf16[512,256]{1,0:T(8,128)(2,1)S(1)} collective-permute-done((bf16[512,256]{1,0:T(8,128)(2,1)S(1)}, bf16[512,256]{1,0:T(8,128)(2,1)S(1)}, u32[]{:S(2)}, u32[]{:S(2)}) %collective-permute-start.15) | collective-permute-done | bytes 262176 | tf_op jit(solution)/shard_map/ppermute | solution.py:41
  176.0 5.2 %collective-permute-start.16 = (bf16[512,256]{1,0:T(8,128)(2,1)S(1)}, bf16[512,256]{1,0:T(8,128)(2,1)S(1)}, u32[]{:S(2)}, u32[]{:S(2)}) collective-permute-start(bf16[512,256]{1,0:T(8,128)(2,1)S(1)} %add_convert_fusion.1), channel_id=1, source_target_pairs={{0,448},{64,0},{128,64},{192,128},{256,192},{320,256},{384,320},{4... | collective-permute-start | bytes 786440 | tf_op jit(solution)/shard_map/ppermute | solution.py:41
  185.5 4.1 %collective-permute-done.14 = bf16[512,256]{1,0:T(8,128)(2,1)S(1)} collective-permute-done((bf16[512,256]{1,0:T(8,128)(2,1)S(1)}, bf16[512,256]{1,0:T(8,128)(2,1)S(1)}, u32[]{:S(2)}, u32[]{:S(2)}) %collective-permute-start.14) | collective-permute-done | bytes 262176 | tf_op jit(solution)/shard_map/ppermute | solution.py:38
  191.5 14.9 %all-to-all-start.2 = ((bf16[64,16,256]{2,1,0:T(8,128)(2,1)}), bf16[64,16,256]{2,1,0:T(8,128)(2,1)S(1)}, u32[]{:S(2)}, u32[]{:S(2)}) async-start(bf16[64,16,256]{2,1,0:T(8,128)(2,1)} %pad_maximum_fusion.3), calls=%async_computation.4 | async-start | bytes 1048576 | tf_op jit(solution)/shard_map/all_to_all | solution.py:172
  206.4 16.8 %reduce-scatter.3.cloned.1.call-done = bf16[512,256]{1,0:T(8,128)(2,1)} async-done(((bf16[512,2048]{1,0:T(8,128)(2,1)}), bf16[512,256]{1,0:T(8,128)(2,1)}) %reduce-scatter.3.cloned.1.call-update) | async-done | bytes 262160 | tf_op jit(solution)/shard_map/reduce_scatter | solution.py:163
  (108 shorter events, 64.1 us)
Async XLA Ops:
  7.2 116.4 %copy-start = (bf16[1,512,2048]{2,1,0:T(8,128)(2,1)S(1)}, bf16[1,512,2048]{2,1,0:T(8,128)(2,1)}, u32[]{:S(2)}) copy-start(bf16[1,512,2048]{2,1,0:T(8,128)(2,1)} %param.15) | copy-start | bytes 6291460
  11.1 29.1 %all-to-all-start = ((bf16[64,16,256]{2,1,0:T(8,128)(2,1)}), bf16[64,16,256]{2,1,0:T(8,128)(2,1)S(1)}, u32[]{:S(2)}, u32[]{:S(2)}) async-start(bf16[64,16,256]{2,1,0:T(8,128)(2,1)} %pad_maximum_fusion.1), calls=%async_computation | async-start | bytes 1048576 | tf_op jit(solution)/shard_map/all_to_all | solution.py:64
  22.9 96.2 %all-gather.2.cloned.1.call-start = ((), (), s32[]{:S(2)}) async-start(), calls=%async_computation.5 | async-start | bytes 4718592 | tf_op jit(solution)/shard_map/all_gather | solution.py:69
  23.0 18.1 %collective-permute-start = (bf16[512,256]{1,0:T(8,128)(2,1)S(1)}, bf16[512,256]{1,0:T(8,128)(2,1)}, u32[]{:S(2)}, u32[]{:S(2)}) collective-permute-start(bf16[512,256]{1,0:T(8,128)(2,1)S(1)} %get-tuple-element.55), channel_id=1, source_target_pairs={{0,64},{64,128},{128,192},{192,256},{256,320},{320,384},{384,448},... | collective-permute-start | bytes 786440 | tf_op jit(solution)/shard_map/ppermute | solution.py:38
  27.0 14.1 %collective-permute-start.1 = (bf16[512,256]{1,0:T(8,128)(2,1)S(1)}, bf16[512,256]{1,0:T(8,128)(2,1)}, u32[]{:S(2)}, u32[]{:S(2)}) collective-permute-start(bf16[512,256]{1,0:T(8,128)(2,1)S(1)} %get-tuple-element.54), channel_id=1, source_target_pairs={{0,448},{64,0},{128,64},{192,128},{256,192},{320,256},{384,320},{4... | collective-permute-start | bytes 786440 | tf_op jit(solution)/shard_map/ppermute | solution.py:41
  42.8 62.4 %all-to-all-start.1 = ((bf16[64,64,256]{2,1,0:T(8,128)(2,1)}), bf16[64,64,256]{2,1,0:T(8,128)(2,1)}, u32[]{:S(2)}, u32[]{:S(2)}) async-start(bf16[64,64,256]{2,1,0:T(8,128)(2,1)} %bitcast.92), calls=%async_computation.1 | async-start | bytes 4194304 | tf_op jit(solution)/shard_map/all_to_all | solution.py:76
  54.0 135.7 %reduce-scatter.5.cloned.1.call-start = ((), (), s32[]{:S(2)}) async-start(), calls=%async_computation.7 | async-start | bytes 2359296 | tf_op jit(solution)/shard_map/reduce_scatter | solution.py:138
  57.0 13.3 %collective-permute-start.3 = (bf16[512,256]{1,0:T(8,128)(2,1)}, bf16[512,256]{1,0:T(8,128)(2,1)S(1)}, u32[]{:S(2)}, u32[]{:S(2)}) collective-permute-start(bf16[512,256]{1,0:T(8,128)(2,1)} %collective-permute-done.1), channel_id=1, source_target_pairs={{0,448},{64,0},{128,64},{192,128},{256,192},{320,256},{384,320},{4... | collective-permute-start | bytes 786440 | tf_op jit(solution)/shard_map/ppermute | solution.py:41
  63.0 15.7 %collective-permute-start.2 = (bf16[512,256]{1,0:T(8,128)(2,1)}, bf16[512,256]{1,0:T(8,128)(2,1)S(1)}, u32[]{:S(2)}, u32[]{:S(2)}) collective-permute-start(bf16[512,256]{1,0:T(8,128)(2,1)} %collective-permute-done), channel_id=1, source_target_pairs={{0,64},{64,128},{128,192},{192,256},{256,320},{320,384},{384,448},... | collective-permute-start | bytes 786440 | tf_op jit(solution)/shard_map/ppermute | solution.py:38
  70.4 24.3 %collective-permute-start.5 = (bf16[512,256]{1,0:T(8,128)(2,1)S(1)}, bf16[512,256]{1,0:T(8,128)(2,1)S(1)}, u32[]{:S(2)}, u32[]{:S(2)}) collective-permute-start(bf16[512,256]{1,0:T(8,128)(2,1)S(1)} %collective-permute-done.3), channel_id=1, source_target_pairs={{0,448},{64,0},{128,64},{192,128},{256,192},{320,256},{384,320},{4... | collective-permute-start | bytes 786440 | tf_op jit(solution)/shard_map/ppermute | solution.py:41
  78.8 13.2 %collective-permute-start.4 = (bf16[512,256]{1,0:T(8,128)(2,1)S(1)}, bf16[512,256]{1,0:T(8,128)(2,1)S(1)}, u32[]{:S(2)}, u32[]{:S(2)}) collective-permute-start(bf16[512,256]{1,0:T(8,128)(2,1)S(1)} %collective-permute-done.2), channel_id=1, source_target_pairs={{0,64},{64,128},{128,192},{192,256},{256,320},{320,384},{384,448},... | collective-permute-start | bytes 786440 | tf_op jit(solution)/shard_map/ppermute | solution.py:38
  92.0 9.0 %collective-permute-start.6 = (bf16[256,256]{1,0:T(8,128)(2,1)S(1)}, bf16[256,256]{1,0:T(8,128)(2,1)S(1)}, u32[]{:S(2)}, u32[]{:S(2)}) collective-permute-start(bf16[256,256]{1,0:T(8,128)(2,1)S(1)} %slice.147), channel_id=1, source_target_pairs={{0,64},{64,128},{128,192},{192,256},{256,320},{320,384},{384,448},... | collective-permute-start | bytes 393224 | tf_op jit(solution)/shard_map/ppermute | solution.py:38
  95.4 9.2 %collective-permute-start.7 = (bf16[256,256]{1,0:T(8,128)(2,1)S(1)}, bf16[256,256]{1,0:T(8,128)(2,1)S(1)}, u32[]{:S(2)}, u32[]{:S(2)}) collective-permute-start(bf16[256,256]{1,0:T(8,128)(2,1)S(1)} %get-tuple-element.52), channel_id=1, source_target_pairs={{0,448},{64,0},{128,64},{192,128},{256,192},{320,256},{384,320},{4... | collective-permute-start | bytes 393224 | tf_op jit(solution)/shard_map/ppermute | solution.py:41
  105.3 25.2 %collective-permute-start.8 = (bf16[64,64,256]{2,1,0:T(8,128)(2,1)}, bf16[64,64,256]{2,1,0:T(8,128)(2,1)}, u32[]{:S(2)}, u32[]{:S(2)}) collective-permute-start(bf16[64,64,256]{2,1,0:T(8,128)(2,1)} %all-to-all-done.1), channel_id=1, source_target_pairs={{0,1},{1,0},{2,3},{3,2},{4,5},{5,4},{6,7},{7,6},{8,9},{9,8},{10,11... | collective-permute-start | bytes 6291464 | tf_op jit(solution)/shard_map/ppermute | solution.py:122
  130.5 92.8 %reduce-scatter.3.cloned.1.call-start = ((), (), s32[]{:S(2)}) async-start(), calls=%async_computation.6 | async-start | bytes 2359296 | tf_op jit(solution)/shard_map/reduce_scatter | solution.py:163
  130.9 13.7 %collective-permute-start.9 = (bf16[256,256]{1,0:T(8,128)(2,1)S(1)}, bf16[256,256]{1,0:T(8,128)(2,1)S(1)}, u32[]{:S(2)}, u32[]{:S(2)}) collective-permute-start(bf16[256,256]{1,0:T(8,128)(2,1)S(1)} %get-tuple-element.51), channel_id=1, source_target_pairs={{0,64},{64,128},{128,192},{192,256},{256,320},{320,384},{384,448},... | collective-permute-start | bytes 393224 | tf_op jit(solution)/shard_map/ppermute | solution.py:38
  134.3 10.4 %collective-permute-start.10 = (bf16[256,256]{1,0:T(8,128)(2,1)S(1)}, bf16[256,256]{1,0:T(8,128)(2,1)S(1)}, u32[]{:S(2)}, u32[]{:S(2)}) collective-permute-start(bf16[256,256]{1,0:T(8,128)(2,1)S(1)} %get-tuple-element.50), channel_id=1, source_target_pairs={{0,448},{64,0},{128,64},{192,128},{256,192},{320,256},{384,320},{4... | collective-permute-start | bytes 393224 | tf_op jit(solution)/shard_map/ppermute | solution.py:41
  145.5 15.0 %collective-permute-start.11 = (bf16[512,256]{1,0:T(8,128)(2,1)S(1)}, bf16[512,256]{1,0:T(8,128)(2,1)}, u32[]{:S(2)}, u32[]{:S(2)}) collective-permute-start(bf16[512,256]{1,0:T(8,128)(2,1)S(1)} %pad_maximum_fusion.6), channel_id=1, source_target_pairs={{0,64},{64,128},{128,192},{192,256},{256,320},{320,384},{384,448},... | collective-permute-start | bytes 786440 | tf_op jit(solution)/shard_map/ppermute | solution.py:38
  147.7 14.0 %collective-permute-start.12 = (bf16[512,256]{1,0:T(8,128)(2,1)}, bf16[512,256]{1,0:T(8,128)(2,1)S(1)}, u32[]{:S(2)}, u32[]{:S(2)}) collective-permute-start(bf16[512,256]{1,0:T(8,128)(2,1)} %pad_maximum_fusion.7), channel_id=1, source_target_pairs={{0,448},{64,0},{128,64},{192,128},{256,192},{320,256},{384,320},{4... | collective-permute-start | bytes 786440 | tf_op jit(solution)/shard_map/ppermute | solution.py:41
  163.7 12.2 %collective-permute-start.15 = (bf16[512,256]{1,0:T(8,128)(2,1)S(1)}, bf16[512,256]{1,0:T(8,128)(2,1)S(1)}, u32[]{:S(2)}, u32[]{:S(2)}) collective-permute-start(bf16[512,256]{1,0:T(8,128)(2,1)S(1)} %copy-done.7), channel_id=1, source_target_pairs={{0,448},{64,0},{128,64},{192,128},{256,192},{320,256},{384,320},{4... | collective-permute-start | bytes 786440 | tf_op jit(solution)/shard_map/ppermute | solution.py:41
  168.1 13.1 %collective-permute-start.13 = (bf16[512,256]{1,0:T(8,128)(2,1)S(1)}, bf16[512,256]{1,0:T(8,128)(2,1)S(1)}, u32[]{:S(2)}, u32[]{:S(2)}) collective-permute-start(bf16[512,256]{1,0:T(8,128)(2,1)S(1)} %add_convert_fusion.4), channel_id=1, source_target_pairs={{0,64},{64,128},{128,192},{192,256},{256,320},{320,384},{384,448},... | collective-permute-start | bytes 786440 | tf_op jit(solution)/shard_map/ppermute | solution.py:38
  176.0 9.5 %collective-permute-start.16 = (bf16[512,256]{1,0:T(8,128)(2,1)S(1)}, bf16[512,256]{1,0:T(8,128)(2,1)S(1)}, u32[]{:S(2)}, u32[]{:S(2)}) collective-permute-start(bf16[512,256]{1,0:T(8,128)(2,1)S(1)} %add_convert_fusion.1), channel_id=1, source_target_pairs={{0,448},{64,0},{128,64},{192,128},{256,192},{320,256},{384,320},{4... | collective-permute-start | bytes 786440 | tf_op jit(solution)/shard_map/ppermute | solution.py:41
  181.3 8.3 %collective-permute-start.14 = (bf16[512,256]{1,0:T(8,128)(2,1)S(1)}, bf16[512,256]{1,0:T(8,128)(2,1)S(1)}, u32[]{:S(2)}, u32[]{:S(2)}) collective-permute-start(bf16[512,256]{1,0:T(8,128)(2,1)S(1)} %add_convert_fusion.2), channel_id=1, source_target_pairs={{0,64},{64,128},{128,192},{192,256},{256,320},{320,384},{384,448},... | collective-permute-start | bytes 786440 | tf_op jit(solution)/shard_map/ppermute | solution.py:38
  191.5 32.7 %all-to-all-start.2 = ((bf16[64,16,256]{2,1,0:T(8,128)(2,1)}), bf16[64,16,256]{2,1,0:T(8,128)(2,1)S(1)}, u32[]{:S(2)}, u32[]{:S(2)}) async-start(bf16[64,16,256]{2,1,0:T(8,128)(2,1)} %pad_maximum_fusion.3), calls=%async_computation.4 | async-start | bytes 1048576 | tf_op jit(solution)/shard_map/all_to_all | solution.py:172
  (10 other events, 139.6 us)
Sparse Core Ops, SparseCore 0:
  41.2 77.8 all-gather.1
  130.6 46.9 reduce-scatter.4
  180.4 42.7 reduce-scatter.2

commit v3 on v2

--- a/solution.py
+++ b/solution.py
@@ -160,7 +160,7 @@
             right, left, dense = lax.optimization_barrier((right, left, dense))
         right, left = to_right(right), to_left(left)
     sum_out = (part_out(0) + right.astype(f32) + left.astype(f32)).astype(bf16)
-    dense_sum = lax.psum_scatter(dense, "node", scatter_dimension=1, tiled=True).astype(f32)
+    dense_sum = lax.psum_scatter(dense, "node", scatter_dimension=1, tiled=True)
 
     reply = jnp.concatenate(
         [
@@ -184,8 +184,11 @@
         preferred_element_type=f32,
     )
     scale = gate[:, None]
-    mixed = tokens.astype(f32) + dense_sum[:tok_count] + scale * picked_out
-    input_grad = cotangent.astype(f32) + dense_sum[tok_count:] + scale * picked_back
+    mixed = tokens.astype(f32) + scale * picked_out
+    input_grad = cotangent.astype(f32) + scale * picked_back
+    mixed, input_grad = lax.optimization_barrier((mixed, input_grad))
+    mixed = mixed + dense_sum[:tok_count].astype(f32)
+    input_grad = input_grad + dense_sum[tok_count:].astype(f32)
     return mixed.astype(bf16), input_grad.astype(bf16)
 
 

time: 238 us -> 235 us (0.987)
  blocking collectives: 0 us -> 30.7 us
  starting transfers between devices: 103 us -> 86.2 us
  waiting for transfers between devices: 58.7 us -> 43.6 us
    all_to_all x0 -> x1, blocking collectives: none -> 30.7 us  [body(): lax.all_to_all(reply, 'outer', split_axis=0, concat_axis=0, tiled=True)]
    reduce_scatter x1, waiting for transfers between devices: 16.8 us -> 0.02 us  [body(): dense_sum = lax.psum_scatter(dense, 'node', scatter_dimension=1, tiled=True)]
    all_to_all x1 -> x0, starting transfers between devices: 14.9 us -> none  [body(): lax.all_to_all(reply, 'outer', split_axis=0, concat_axis=0, tiled=True)]
  transfers between devices with their start and end apart: 23 -> 22, of which waited for: 12 -> 11; matrix products, arithmetic and copies ran while one was open for 21% -> 21% of each run, Pallas kernels for 0% -> 0%
where the time goes in v3:
time: 235 us; the launch traced here: 231 us
  starting transfers between devices  86.2 us (37%)
  waiting for transfers between devices  43.6 us (19%)
  blocking collectives  30.7 us (13%)
  matrix products  26.8 us (11%)
  local copies, waits for them, and re-layouts  21.3 us (9%)
  between operations  14.3 us (6%)
  other arithmetic  8.39 us (4%)
    ppermute x8, starting transfers between devices, to_left(): lax.ppermute(a, 'node', [(i, (i - 1) % n_node) for i in range(n_node)])  39.8 us
    all_to_all x1, blocking collectives, body(): lax.all_to_all(reply, 'outer', split_axis=0, concat_axis=0, tiled=True)  30.7 us
    ppermute x8, waiting for transfers between devices, to_right(): lax.ppermute(a, 'node', [(i, (i + 1) % n_node) for i in range(n_node)])  24.6 us
    ppermute x8, starting transfers between devices, to_right(): lax.ppermute(a, 'node', [(i, (i + 1) % n_node) for i in range(n_node)])  19.3 us
    dot_general x15, matrix products, dot(): return jnp.dot(left, right, preferred_element_type=jnp.float32)  17.7 us
    all_to_all x1, starting transfers between devices, body(): own = lax.all_to_all(send, 'outer', split_axis=0, concat_axis=0, tiled=True)  11.8 us
    all_to_all x1, starting transfers between devices, body(): lax.all_to_all(pieces.reshape(n_outer, 2 * depth, width // 2), 'outer', s...  11.1 us
    dynamic_update_slice x12, local copies, waits for them, and re-layouts, put(): lax.dynamic_update_slice(array, values, (jnp.uint32(row), start_of(offset)))  11.1 us
  transfers between devices with their start and end apart: 22, of which 11 were waited for; matrix products, arithmetic and copies ran while one was open for 21% of the time, Pallas kernels for 0%

profile of v3, /device:TPU:1, one launch (start us, length us, event | category | flops | bytes accessed | tf_op | source)
XLA Modules:
  0.0 231.4 jit_solution(8469624716959221032)
XLA Ops:
  11.1 11.8 %all-to-all-start = ((bf16[64,16,256]{2,1,0:T(8,128)(2,1)}), bf16[64,16,256]{2,1,0:T(8,128)(2,1)S(1)}, u32[]{:S(2)}, u32[]{:S(2)}) async-start(bf16[64,16,256]{2,1,0:T(8,128)(2,1)} %pad_maximum_fusion.1), calls=%async_computation | async-start | bytes 1048576 | tf_op jit(solution)/shard_map/all_to_all | solution.py:64
  23.0 4.0 %collective-permute-start = (bf16[512,256]{1,0:T(8,128)(2,1)S(1)}, bf16[512,256]{1,0:T(8,128)(2,1)}, u32[]{:S(2)}, u32[]{:S(2)}) collective-permute-start(bf16[512,256]{1,0:T(8,128)(2,1)S(1)} %get-tuple-element.61), channel_id=1, source_target_pairs={{0,64},{64,128},{128,192},{192,256},{256,320},{320,384},{384,448},... | collective-permute-start | bytes 786440 | tf_op jit(solution)/shard_map/ppermute | solution.py:38
  27.0 8.6 %collective-permute-start.1 = (bf16[512,256]{1,0:T(8,128)(2,1)S(1)}, bf16[512,256]{1,0:T(8,128)(2,1)}, u32[]{:S(2)}, u32[]{:S(2)}) collective-permute-start(bf16[512,256]{1,0:T(8,128)(2,1)S(1)} %get-tuple-element.60), channel_id=1, source_target_pairs={{0,448},{64,0},{128,64},{192,128},{256,192},{320,256},{384,320},{4... | collective-permute-start | bytes 786440 | tf_op jit(solution)/shard_map/ppermute | solution.py:41
  35.6 4.6 %all-to-all-done = bf16[64,16,256]{2,1,0:T(8,128)(2,1)S(1)} async-done(((bf16[64,16,256]{2,1,0:T(8,128)(2,1)}), bf16[64,16,256]{2,1,0:T(8,128)(2,1)S(1)}, u32[]{:S(2)}, u32[]{:S(2)}) %all-to-all-start) | async-done | bytes 524320 | tf_op jit(solution)/shard_map/all_to_all | solution.py:64
  42.8 11.1 %all-to-all-start.1 = ((bf16[64,64,256]{2,1,0:T(8,128)(2,1)}), bf16[64,64,256]{2,1,0:T(8,128)(2,1)}, u32[]{:S(2)}, u32[]{:S(2)}) async-start(bf16[64,64,256]{2,1,0:T(8,128)(2,1)} %bitcast.92), calls=%async_computation.1 | async-start | bytes 4194304 | tf_op jit(solution)/shard_map/all_to_all | solution.py:76
  57.1 6.0 %collective-permute-start.3 = (bf16[512,256]{1,0:T(8,128)(2,1)}, bf16[512,256]{1,0:T(8,128)(2,1)S(1)}, u32[]{:S(2)}, u32[]{:S(2)}) collective-permute-start(bf16[512,256]{1,0:T(8,128)(2,1)} %collective-permute-done.1), channel_id=1, source_target_pairs={{0,448},{64,0},{128,64},{192,128},{256,192},{320,256},{384,320},{4... | collective-permute-start | bytes 786440 | tf_op jit(solution)/shard_map/ppermute | solution.py:41
  70.3 5.3 %collective-permute-start.5 = (bf16[512,256]{1,0:T(8,128)(2,1)S(1)}, bf16[512,256]{1,0:T(8,128)(2,1)S(1)}, u32[]{:S(2)}, u32[]{:S(2)}) collective-permute-start(bf16[512,256]{1,0:T(8,128)(2,1)S(1)} %collective-permute-done.3), channel_id=1, source_target_pairs={{0,448},{64,0},{128,64},{192,128},{256,192},{320,256},{384,320},{4... | collective-permute-start | bytes 786440 | tf_op jit(solution)/shard_map/ppermute | solution.py:41
  75.6 3.2 %collective-permute-done.2 = bf16[512,256]{1,0:T(8,128)(2,1)S(1)} collective-permute-done((bf16[512,256]{1,0:T(8,128)(2,1)}, bf16[512,256]{1,0:T(8,128)(2,1)S(1)}, u32[]{:S(2)}, u32[]{:S(2)}) %collective-permute-start.2) | collective-permute-done | bytes 262176 | tf_op jit(solution)/shard_map/ppermute | solution.py:38
  82.8 9.2 %collective-permute-done.4 = bf16[512,256]{1,0:T(8,128)(2,1)S(1)} collective-permute-done((bf16[512,256]{1,0:T(8,128)(2,1)S(1)}, bf16[512,256]{1,0:T(8,128)(2,1)S(1)}, u32[]{:S(2)}, u32[]{:S(2)}) %collective-permute-start.4) | collective-permute-done | bytes 262176 | tf_op jit(solution)/shard_map/ppermute | solution.py:38
  95.4 4.5 %collective-permute-start.7 = (bf16[256,256]{1,0:T(8,128)(2,1)S(1)}, bf16[256,256]{1,0:T(8,128)(2,1)S(1)}, u32[]{:S(2)}, u32[]{:S(2)}) collective-permute-start(bf16[256,256]{1,0:T(8,128)(2,1)S(1)} %get-tuple-element.58), channel_id=1, source_target_pairs={{0,448},{64,0},{128,64},{192,128},{256,192},{320,256},{384,320},{4... | collective-permute-start | bytes 393224 | tf_op jit(solution)/shard_map/ppermute | solution.py:41
  101.7 2.9 %collective-permute-done.7 = bf16[256,256]{1,0:T(8,128)(2,1)S(1)} collective-permute-done((bf16[256,256]{1,0:T(8,128)(2,1)S(1)}, bf16[256,256]{1,0:T(8,128)(2,1)S(1)}, u32[]{:S(2)}, u32[]{:S(2)}) %collective-permute-start.7) | collective-permute-done | bytes 131104 | tf_op jit(solution)/shard_map/ppermute | solution.py:41
  105.3 4.0 %collective-permute-start.8 = (bf16[64,64,256]{2,1,0:T(8,128)(2,1)}, bf16[64,64,256]{2,1,0:T(8,128)(2,1)}, u32[]{:S(2)}, u32[]{:S(2)}) collective-permute-start(bf16[64,64,256]{2,1,0:T(8,128)(2,1)} %all-to-all-done.1), channel_id=1, source_target_pairs={{0,1},{1,0},{2,3},{3,2},{4,5},{5,4},{6,7},{7,6},{8,9},{9,8},{10,11... | collective-permute-start | bytes 6291464 | tf_op jit(solution)/shard_map/ppermute | solution.py:122
  115.4 3.7 %all-gather.2.cloned.1.call-done = bf16[1024,2048]{1,0:T(8,128)(2,1)} async-done(((bf16[1024,256]{1,0:T(8,128)(2,1)}), bf16[1024,2048]{1,0:T(8,128)(2,1)}) %all-gather.2.cloned.1.call-update) | async-done | bytes 4194320 | tf_op jit(solution)/shard_map/all_gather | solution.py:69
  119.2 4.5 %multiply_convert_fusion = (bf16[512,512]{1,0:T(8,128)(2,1)S(1)}, f32[512,512]{1,0:T(8,128)}) fusion(bf16[1,2048,512]{2,1,0:T(8,128)(2,1)} %param.14, bf16[1024,2048]{1,0:T(8,128)(2,1)} %all-gather.2.cloned.1.call-done), kind=kOutput, calls=%fused_computation.38 | convolution fusion | flops 1075052544 | bytes 5767168 | tf_op jit(solution)/shard_map/dot_general | solution.py:19
  124.0 6.5 %convolution_convert_fusion = bf16[512,2048]{1,0:T(8,128)(2,1)} fusion(bf16[1,2048,512]{2,1,0:T(8,128)(2,1)} %param.14, bf16[1,512,2048]{2,1,0:T(8,128)(2,1)S(1)} %copy-done, bf16[1024,2048]{1,0:T(8,128)(2,1)} %all-gather.2.cloned.1.call-done, f32[512,512]{1,0:T(8,128)} %get-tuple-element.67), kind=kOutput, calls=%fused_computation | convolution fusion | flops 2151153664 | bytes 9437184 | tf_op jit(solution)/shard_map/dot_general | solution.py:23
  130.9 3.4 %collective-permute-start.9 = (bf16[256,256]{1,0:T(8,128)(2,1)S(1)}, bf16[256,256]{1,0:T(8,128)(2,1)S(1)}, u32[]{:S(2)}, u32[]{:S(2)}) collective-permute-start(bf16[256,256]{1,0:T(8,128)(2,1)S(1)} %get-tuple-element.57), channel_id=1, source_target_pairs={{0,64},{64,128},{128,192},{192,256},{256,320},{320,384},{384,448},... | collective-permute-start | bytes 393224 | tf_op jit(solution)/shard_map/ppermute | solution.py:38
  134.4 3.1 %collective-permute-start.10 = (bf16[256,256]{1,0:T(8,128)(2,1)S(1)}, bf16[256,256]{1,0:T(8,128)(2,1)S(1)}, u32[]{:S(2)}, u32[]{:S(2)}) collective-permute-start(bf16[256,256]{1,0:T(8,128)(2,1)S(1)} %get-tuple-element.56), channel_id=1, source_target_pairs={{0,448},{64,0},{128,64},{192,128},{256,192},{320,256},{384,320},{4... | collective-permute-start | bytes 393224 | tf_op jit(solution)/shard_map/ppermute | solution.py:41
  148.5 4.4 %collective-permute-start.12 = (bf16[512,256]{1,0:T(8,128)(2,1)}, bf16[512,256]{1,0:T(8,128)(2,1)S(1)}, u32[]{:S(2)}, u32[]{:S(2)}) collective-permute-start(bf16[512,256]{1,0:T(8,128)(2,1)} %pad_maximum_fusion.7), channel_id=1, source_target_pairs={{0,448},{64,0},{128,64},{192,128},{256,192},{320,256},{384,320},{4... | collective-permute-start | bytes 786440 | tf_op jit(solution)/shard_map/ppermute | solution.py:41
  155.4 6.7 %collective-permute-done.11 = bf16[512,256]{1,0:T(8,128)(2,1)} collective-permute-done((bf16[512,256]{1,0:T(8,128)(2,1)}, bf16[512,256]{1,0:T(8,128)(2,1)}, u32[]{:S(2)}, u32[]{:S(2)}) %collective-permute-start.11) | collective-permute-done | bytes 262176 | tf_op jit(solution)/shard_map/ppermute | solution.py:38
  165.3 3.3 %collective-permute-start.15 = (bf16[512,256]{1,0:T(8,128)(2,1)S(1)}, bf16[512,256]{1,0:T(8,128)(2,1)S(1)}, u32[]{:S(2)}, u32[]{:S(2)}) collective-permute-start(bf16[512,256]{1,0:T(8,128)(2,1)S(1)} %copy-done.7), channel_id=1, source_target_pairs={{0,448},{64,0},{128,64},{192,128},{256,192},{320,256},{384,320},{4... | collective-permute-start | bytes 786440 | tf_op jit(solution)/shard_map/ppermute | solution.py:41
  171.3 6.2 %collective-permute-done.15 = bf16[512,256]{1,0:T(8,128)(2,1)S(1)} collective-permute-done((bf16[512,256]{1,0:T(8,128)(2,1)S(1)}, bf16[512,256]{1,0:T(8,128)(2,1)S(1)}, u32[]{:S(2)}, u32[]{:S(2)}) %collective-permute-start.15) | collective-permute-done | bytes 262176 | tf_op jit(solution)/shard_map/ppermute | solution.py:41
  177.5 4.7 %collective-permute-start.16 = (bf16[512,256]{1,0:T(8,128)(2,1)S(1)}, bf16[512,256]{1,0:T(8,128)(2,1)S(1)}, u32[]{:S(2)}, u32[]{:S(2)}) collective-permute-start(bf16[512,256]{1,0:T(8,128)(2,1)S(1)} %add_convert_fusion.1), channel_id=1, source_target_pairs={{0,448},{64,0},{128,64},{192,128},{256,192},{320,256},{384,320},{4... | collective-permute-start | bytes 786440 | tf_op jit(solution)/shard_map/ppermute | solution.py:41
  185.5 5.1 %collective-permute-done.14 = bf16[512,256]{1,0:T(8,128)(2,1)S(1)} collective-permute-done((bf16[512,256]{1,0:T(8,128)(2,1)S(1)}, bf16[512,256]{1,0:T(8,128)(2,1)S(1)}, u32[]{:S(2)}, u32[]{:S(2)}) %collective-permute-start.14) | collective-permute-done | bytes 262176 | tf_op jit(solution)/shard_map/ppermute | solution.py:38
  191.7 30.7 %all_to_all.15 = bf16[64,16,256]{2,1,0:T(8,128)(2,1)S(1)} all-to-all(bf16[64,16,256]{2,1,0:T(8,128)(2,1)S(1)} %pad_maximum_fusion.3), channel_id=1, replica_groups=mesh['node'=8,'outer'=64] {'outer'}, dimensions={0} | all-to-all | bytes 1048576 | tf_op jit(solution)/shard_map/all_to_all | solution.py:172
  (107 shorter events, 59.6 us)
Async XLA Ops:
  7.2 116.5 %copy-start = (bf16[1,512,2048]{2,1,0:T(8,128)(2,1)S(1)}, bf16[1,512,2048]{2,1,0:T(8,128)(2,1)}, u32[]{:S(2)}) copy-start(bf16[1,512,2048]{2,1,0:T(8,128)(2,1)} %param.15) | copy-start | bytes 6291460
  11.1 29.1 %all-to-all-start = ((bf16[64,16,256]{2,1,0:T(8,128)(2,1)}), bf16[64,16,256]{2,1,0:T(8,128)(2,1)S(1)}, u32[]{:S(2)}, u32[]{:S(2)}) async-start(bf16[64,16,256]{2,1,0:T(8,128)(2,1)} %pad_maximum_fusion.1), calls=%async_computation | async-start | bytes 1048576 | tf_op jit(solution)/shard_map/all_to_all | solution.py:64
  22.9 96.3 %all-gather.2.cloned.1.call-start = ((), (), s32[]{:S(2)}) async-start(), calls=%async_computation.5 | async-start | bytes 4718592 | tf_op jit(solution)/shard_map/all_gather | solution.py:69
  23.0 18.1 %collective-permute-start = (bf16[512,256]{1,0:T(8,128)(2,1)S(1)}, bf16[512,256]{1,0:T(8,128)(2,1)}, u32[]{:S(2)}, u32[]{:S(2)}) collective-permute-start(bf16[512,256]{1,0:T(8,128)(2,1)S(1)} %get-tuple-element.61), channel_id=1, source_target_pairs={{0,64},{64,128},{128,192},{192,256},{256,320},{320,384},{384,448},... | collective-permute-start | bytes 786440 | tf_op jit(solution)/shard_map/ppermute | solution.py:38
  27.0 14.1 %collective-permute-start.1 = (bf16[512,256]{1,0:T(8,128)(2,1)S(1)}, bf16[512,256]{1,0:T(8,128)(2,1)}, u32[]{:S(2)}, u32[]{:S(2)}) collective-permute-start(bf16[512,256]{1,0:T(8,128)(2,1)S(1)} %get-tuple-element.60), channel_id=1, source_target_pairs={{0,448},{64,0},{128,64},{192,128},{256,192},{320,256},{384,320},{4... | collective-permute-start | bytes 786440 | tf_op jit(solution)/shard_map/ppermute | solution.py:41
  42.8 62.5 %all-to-all-start.1 = ((bf16[64,64,256]{2,1,0:T(8,128)(2,1)}), bf16[64,64,256]{2,1,0:T(8,128)(2,1)}, u32[]{:S(2)}, u32[]{:S(2)}) async-start(bf16[64,64,256]{2,1,0:T(8,128)(2,1)} %bitcast.92), calls=%async_computation.1 | async-start | bytes 4194304 | tf_op jit(solution)/shard_map/all_to_all | solution.py:76
  54.0 136.7 %reduce-scatter.3.cloned.1.call-start = ((), (), s32[]{:S(2)}) async-start(), calls=%async_computation.6 | async-start | bytes 2359296 | tf_op jit(solution)/shard_map/reduce_scatter | solution.py:138
  57.1 13.2 %collective-permute-start.3 = (bf16[512,256]{1,0:T(8,128)(2,1)}, bf16[512,256]{1,0:T(8,128)(2,1)S(1)}, u32[]{:S(2)}, u32[]{:S(2)}) collective-permute-start(bf16[512,256]{1,0:T(8,128)(2,1)} %collective-permute-done.1), channel_id=1, source_target_pairs={{0,448},{64,0},{128,64},{192,128},{256,192},{320,256},{384,320},{4... | collective-permute-start | bytes 786440 | tf_op jit(solution)/shard_map/ppermute | solution.py:41
  63.0 15.8 %collective-permute-start.2 = (bf16[512,256]{1,0:T(8,128)(2,1)}, bf16[512,256]{1,0:T(8,128)(2,1)S(1)}, u32[]{:S(2)}, u32[]{:S(2)}) collective-permute-start(bf16[512,256]{1,0:T(8,128)(2,1)} %collective-permute-done), channel_id=1, source_target_pairs={{0,64},{64,128},{128,192},{192,256},{256,320},{320,384},{384,448},... | collective-permute-start | bytes 786440 | tf_op jit(solution)/shard_map/ppermute | solution.py:38
  70.3 24.4 %collective-permute-start.5 = (bf16[512,256]{1,0:T(8,128)(2,1)S(1)}, bf16[512,256]{1,0:T(8,128)(2,1)S(1)}, u32[]{:S(2)}, u32[]{:S(2)}) collective-permute-start(bf16[512,256]{1,0:T(8,128)(2,1)S(1)} %collective-permute-done.3), channel_id=1, source_target_pairs={{0,448},{64,0},{128,64},{192,128},{256,192},{320,256},{384,320},{4... | collective-permute-start | bytes 786440 | tf_op jit(solution)/shard_map/ppermute | solution.py:41
  78.8 13.2 %collective-permute-start.4 = (bf16[512,256]{1,0:T(8,128)(2,1)S(1)}, bf16[512,256]{1,0:T(8,128)(2,1)S(1)}, u32[]{:S(2)}, u32[]{:S(2)}) collective-permute-start(bf16[512,256]{1,0:T(8,128)(2,1)S(1)} %collective-permute-done.2), channel_id=1, source_target_pairs={{0,64},{64,128},{128,192},{192,256},{256,320},{320,384},{384,448},... | collective-permute-start | bytes 786440 | tf_op jit(solution)/shard_map/ppermute | solution.py:38
  92.0 9.0 %collective-permute-start.6 = (bf16[256,256]{1,0:T(8,128)(2,1)S(1)}, bf16[256,256]{1,0:T(8,128)(2,1)S(1)}, u32[]{:S(2)}, u32[]{:S(2)}) collective-permute-start(bf16[256,256]{1,0:T(8,128)(2,1)S(1)} %slice.147), channel_id=1, source_target_pairs={{0,64},{64,128},{128,192},{192,256},{256,320},{320,384},{384,448},... | collective-permute-start | bytes 393224 | tf_op jit(solution)/shard_map/ppermute | solution.py:38
  95.4 9.3 %collective-permute-start.7 = (bf16[256,256]{1,0:T(8,128)(2,1)S(1)}, bf16[256,256]{1,0:T(8,128)(2,1)S(1)}, u32[]{:S(2)}, u32[]{:S(2)}) collective-permute-start(bf16[256,256]{1,0:T(8,128)(2,1)S(1)} %get-tuple-element.58), channel_id=1, source_target_pairs={{0,448},{64,0},{128,64},{192,128},{256,192},{320,256},{384,320},{4... | collective-permute-start | bytes 393224 | tf_op jit(solution)/shard_map/ppermute | solution.py:41
  105.3 25.2 %collective-permute-start.8 = (bf16[64,64,256]{2,1,0:T(8,128)(2,1)}, bf16[64,64,256]{2,1,0:T(8,128)(2,1)}, u32[]{:S(2)}, u32[]{:S(2)}) collective-permute-start(bf16[64,64,256]{2,1,0:T(8,128)(2,1)} %all-to-all-done.1), channel_id=1, source_target_pairs={{0,1},{1,0},{2,3},{3,2},{4,5},{5,4},{6,7},{7,6},{8,9},{9,8},{10,11... | collective-permute-start | bytes 6291464 | tf_op jit(solution)/shard_map/ppermute | solution.py:122
  130.5 92.6 %reduce-scatter.5.cloned.1.call-start = ((), (), s32[]{:S(2)}) async-start(), calls=%async_computation.7 | async-start | bytes 2359296 | tf_op jit(solution)/shard_map/reduce_scatter | solution.py:163
  130.9 13.8 %collective-permute-start.9 = (bf16[256,256]{1,0:T(8,128)(2,1)S(1)}, bf16[256,256]{1,0:T(8,128)(2,1)S(1)}, u32[]{:S(2)}, u32[]{:S(2)}) collective-permute-start(bf16[256,256]{1,0:T(8,128)(2,1)S(1)} %get-tuple-element.57), channel_id=1, source_target_pairs={{0,64},{64,128},{128,192},{192,256},{256,320},{320,384},{384,448},... | collective-permute-start | bytes 393224 | tf_op jit(solution)/shard_map/ppermute | solution.py:38
  134.4 11.1 %collective-permute-start.10 = (bf16[256,256]{1,0:T(8,128)(2,1)S(1)}, bf16[256,256]{1,0:T(8,128)(2,1)S(1)}, u32[]{:S(2)}, u32[]{:S(2)}) collective-permute-start(bf16[256,256]{1,0:T(8,128)(2,1)S(1)} %get-tuple-element.56), channel_id=1, source_target_pairs={{0,448},{64,0},{128,64},{192,128},{256,192},{320,256},{384,320},{4... | collective-permute-start | bytes 393224 | tf_op jit(solution)/shard_map/ppermute | solution.py:41
  146.3 15.8 %collective-permute-start.11 = (bf16[512,256]{1,0:T(8,128)(2,1)}, bf16[512,256]{1,0:T(8,128)(2,1)}, u32[]{:S(2)}, u32[]{:S(2)}) collective-permute-start(bf16[512,256]{1,0:T(8,128)(2,1)} %pad_maximum_fusion.6), channel_id=1, source_target_pairs={{0,64},{64,128},{128,192},{192,256},{256,320},{320,384},{384,448},... | collective-permute-start | bytes 786440 | tf_op jit(solution)/shard_map/ppermute | solution.py:38
  148.5 14.9 %collective-permute-start.12 = (bf16[512,256]{1,0:T(8,128)(2,1)}, bf16[512,256]{1,0:T(8,128)(2,1)S(1)}, u32[]{:S(2)}, u32[]{:S(2)}) collective-permute-start(bf16[512,256]{1,0:T(8,128)(2,1)} %pad_maximum_fusion.7), channel_id=1, source_target_pairs={{0,448},{64,0},{128,64},{192,128},{256,192},{320,256},{384,320},{4... | collective-permute-start | bytes 786440 | tf_op jit(solution)/shard_map/ppermute | solution.py:41
  165.3 12.1 %collective-permute-start.15 = (bf16[512,256]{1,0:T(8,128)(2,1)S(1)}, bf16[512,256]{1,0:T(8,128)(2,1)S(1)}, u32[]{:S(2)}, u32[]{:S(2)}) collective-permute-start(bf16[512,256]{1,0:T(8,128)(2,1)S(1)} %copy-done.7), channel_id=1, source_target_pairs={{0,448},{64,0},{128,64},{192,128},{256,192},{320,256},{384,320},{4... | collective-permute-start | bytes 786440 | tf_op jit(solution)/shard_map/ppermute | solution.py:41
  168.9 13.2 %collective-permute-start.13 = (bf16[512,256]{1,0:T(8,128)(2,1)S(1)}, bf16[512,256]{1,0:T(8,128)(2,1)S(1)}, u32[]{:S(2)}, u32[]{:S(2)}) collective-permute-start(bf16[512,256]{1,0:T(8,128)(2,1)S(1)} %add_convert_fusion.4), channel_id=1, source_target_pairs={{0,64},{64,128},{128,192},{192,256},{256,320},{320,384},{384,448},... | collective-permute-start | bytes 786440 | tf_op jit(solution)/shard_map/ppermute | solution.py:38
  177.5 8.0 %collective-permute-start.16 = (bf16[512,256]{1,0:T(8,128)(2,1)S(1)}, bf16[512,256]{1,0:T(8,128)(2,1)S(1)}, u32[]{:S(2)}, u32[]{:S(2)}) collective-permute-start(bf16[512,256]{1,0:T(8,128)(2,1)S(1)} %add_convert_fusion.1), channel_id=1, source_target_pairs={{0,448},{64,0},{128,64},{192,128},{256,192},{320,256},{384,320},{4... | collective-permute-start | bytes 786440 | tf_op jit(solution)/shard_map/ppermute | solution.py:41
  182.3 40.2 %copy-start.10 = (f32[256]{0:T(256)S(1)}, f32[256]{0:T(256)}, u32[]{:S(2)}) copy-start(f32[256]{0:T(256)} %param.10) | copy-start | bytes 3076
  182.3 8.3 %collective-permute-start.14 = (bf16[512,256]{1,0:T(8,128)(2,1)S(1)}, bf16[512,256]{1,0:T(8,128)(2,1)S(1)}, u32[]{:S(2)}, u32[]{:S(2)}) collective-permute-start(bf16[512,256]{1,0:T(8,128)(2,1)S(1)} %add_convert_fusion.2), channel_id=1, source_target_pairs={{0,64},{64,128},{128,192},{192,256},{256,320},{320,384},{384,448},... | collective-permute-start | bytes 786440 | tf_op jit(solution)/shard_map/ppermute | solution.py:38
  (9 other events, 99.1 us)
Sparse Core Ops, SparseCore 0:
  41.2 77.8 all-gather.1
  130.7 45.7 reduce-scatter.2
  179.2 43.1 reduce-scatter.4
